TPU v7x, 256 devices: a whole 4x4x8 slice. The times are simulated.
256 devices in a mesh: dp: 16 (over z, core), tp: 16 (over x, y).
Axes of the slice: x: 4, y: 4, z: 8, core: 2. Of those that a mesh axis runs over, the one named last changes fastest.
Arguments:
- latent_cache: bfloat16 [1024, 1024, 576], P(('dp', 'tp')), may hold values from -5 to 5
- lengths: int32 [1024], P(('dp', 'tp')), may hold values from 1 to 1022, as said below
- queries: bfloat16 [2, 1024, 128, 576], P(None, ('dp', 'tp')), may hold values from -45 to 45
- new_latents: bfloat16 [2, 1024, 576], P(None, ('dp', 'tp')), may hold values from -5.4 to 5.4
- migrations: int32 [256, 2], P(('dp', 'tp')), may hold values from 0 to 15, as said below
- value_weight: bfloat16 [128, 512, 128], P('tp'), may hold values from -0.25 to 0.25
- output_weight: bfloat16 [16384, 7168], P('tp', 'dp'), may hold values from -0.046875 to 0.046875
Outputs:
- projected: bfloat16 [2560, 7168], P('tp', 'dp')
Inputs may be any that keep to these rules, and one draw needn't show every extreme that they name: `lengths`: A request that migrates holds at most 256 cached positions; in every draw one holds exactly 256, another request exactly 1022, another exactly 1. migrations[d, 0] is 4 where device d hands nothing away; migrations[d, 1] then means nothing. A request moves only between devices of the same tp index and to another dp index; each device takes at most one request; every tp index has a device that hands one away.
All inputs are finite; a program needn't handle non-finite values.
Results may differ from a plain program's by a relative error of at most 0.019.
Values may be sent and summed in bfloat16 or wider, within the bound.
No kernel may reach another device: no remote copies, remote signals or barrier semaphores. Data moves between devices by JAX's collectives and lax.ppermute only.
A program may use at most 64 MiB of HBM per device.

v0:
```python
import math

import jax
import jax.numpy as jnp
from jax import lax
from jax.sharding import PartitionSpec as P

NOPE = 128
ROPE = 64
VAL = 512


def attend_one(request_query, request_cache, request_new, filled):
    scaling = 1.0 / math.sqrt(NOPE + ROPE)
    far_scores = (
        jnp.einsum("shl,cl->shc", request_query, request_cache, preferred_element_type=jnp.float32)
        * scaling
    )
    own_scores = (
        jnp.einsum("shl,tl->sht", request_query, request_new, preferred_element_type=jnp.float32)
        * scaling
    )
    step_count = request_query.shape[0]
    far_mask = (jnp.arange(request_cache.shape[0]) < filled)[None, None, :]
    own_mask = (jnp.arange(step_count)[None, :] <= jnp.arange(step_count)[:, None])[:, None, :]
    highest = jnp.maximum(
        jnp.max(jnp.where(far_mask, far_scores, -jnp.inf), axis=2),
        jnp.max(jnp.where(own_mask, own_scores, -jnp.inf), axis=2),
    )
    far_weights = jnp.where(far_mask, jnp.exp(far_scores - highest[:, :, None]), 0.0)
    own_weights = jnp.where(own_mask, jnp.exp(own_scores - highest[:, :, None]), 0.0)
    denominator = jnp.sum(far_weights, axis=2) + jnp.sum(own_weights, axis=2)
    weighted = jnp.einsum(
        "shc,cv->shv",
        far_weights.astype(jnp.bfloat16),
        request_cache[:, :VAL],
        preferred_element_type=jnp.float32,
    )
    weighted = weighted + jnp.einsum(
        "sht,tv->shv",
        own_weights.astype(jnp.bfloat16),
        request_new[:, :VAL],
        preferred_element_type=jnp.float32,
    )
    return (weighted / denominator[:, :, None]).astype(jnp.bfloat16)


def shards(latent_cache, lengths, queries, new_latents, migrations, value_weight, output_weight):
    requests = latent_cache.shape[0]
    moved_rows = latent_cache.shape[1] // 4
    dp_count = lax.axis_size("dp")
    resident = jax.vmap(attend_one, in_axes=(1, 0, 1, 0), out_axes=1)(
        queries, latent_cache, new_latents, lengths
    )
    outward = migrations[0, 0]
    target = migrations[0, 1]
    leaving = outward < requests
    picked = jnp.minimum(outward, requests - 1)
    taker_code = jnp.where(leaving, target, -1).reshape(1)
    length_sent = lengths[picked].reshape(1)
    my_index = lax.axis_index("dp")
    retained = (jnp.arange(requests) != outward).astype(jnp.bfloat16)
    sent_cache = lax.dynamic_index_in_dim(latent_cache, picked, 0, keepdims=False)[:moved_rows]
    sent_query = lax.dynamic_index_in_dim(queries, picked, 1, keepdims=False)
    sent_new = lax.dynamic_index_in_dim(new_latents, picked, 1, keepdims=False)
    got_cache, got_query, got_new, got_count, got_taker = (
        lax.all_gather(sent_cache[None], "dp", axis=0, tiled=True),
        lax.all_gather(sent_query[None], "dp", axis=0, tiled=True),
        lax.all_gather(sent_new[None], "dp", axis=0, tiled=True),
        lax.all_gather(length_sent, "dp", axis=0, tiled=True),
        lax.all_gather(taker_code, "dp", axis=0, tiled=True),
    )
    arrived = got_taker == my_index
    source = jnp.sum(jnp.where(arrived, jnp.arange(dp_count), 0))
    present = jnp.any(arrived).astype(jnp.bfloat16)
    incoming = (
        attend_one(got_query[source], got_cache[source], got_new[source], got_count[source])
        * present
    )
    slot_rows = jnp.concatenate(
        [resident * retained[None, :, None, None], incoming[:, None]], axis=1
    )
    values_out = jnp.einsum(
        "krhv,hvd->krhd",
        lax.all_to_all(slot_rows, "tp", split_axis=2, concat_axis=1, tiled=True),
        value_weight,
        preferred_element_type=jnp.float32,
    ).astype(jnp.bfloat16)
    lifted = values_out.reshape(
        values_out.shape[0], values_out.shape[1], values_out.shape[2] * values_out.shape[3]
    )
    flattened = lifted.reshape(lifted.shape[0] * lifted.shape[1], lifted.shape[2])
    gathered = lax.all_gather(flattened, "dp", axis=0, tiled=True)
    return lax.psum_scatter(
        jnp.dot(gathered, output_weight, preferred_element_type=jnp.float32).astype(jnp.bfloat16),
        "tp",
        scatter_dimension=0,
        tiled=True,
    )


def solution(mesh):
    return jax.shard_map(
        shards,
        mesh=mesh,
        in_specs=(
            P(("dp", "tp"), None, None),
            P(("dp", "tp")),
            P(None, ("dp", "tp"), None, None),
            P(None, ("dp", "tp"), None),
            P(("dp", "tp"), None),
            P("tp", None, None),
            P("tp", "dp"),
        ),
        out_specs=P("tp", "dp"),
        check_vma=False,
    )
```

profile of v0, /device:TPU:1, one launch (start us, length us, event | category | flops | bytes accessed | tf_op | source)
XLA Modules:
  0.0 263.9 jit_solution(3337486495829720496)
XLA Ops:
  6.5 1.3 fusion.56
  8.6 1.7 constant_dynamic-slice_fusion.3
  10.3 1.7 constant_dynamic-slice_fusion.2
  12.8 1.3 dynamic-slice
  14.8 0.7 dynamic-update-slice.1
  15.5 1.5 dynamic-slice_dynamic-update-slice_fusion
  17.0 14.8 %all-reduce.2 = (s32[16]{0:T(128)S(1)}, s32[16]{0:T(128)S(1)}) all-reduce(s32[16]{0:T(128)S(1)} %dynamic-update-slice.1, s32[16]{0:T(128)S(1)} %dynamic-slice_dynamic-update-slice_fusion), channel_id=1, replica_groups=mesh['dp'=16,'tp'=16] {'dp'}, use_global_device_ids=true, to_apply=%add.1 | all-reduce | flops 32 | bytes 256
  36.4 18.4 %all-gather.1 = bf16[32,1,576]{2,1,0:T(2,128)(2,1)S(1)} all-gather(bf16[2,1,576]{2,1,0:T(2,128)(2,1)S(1)} %constant_dynamic-slice_fusion.1), channel_id=3, replica_groups=mesh['dp'=16,'tp'=16] {'dp'}, dimensions={0}, use_global_device_ids=true | all-gather | bytes 39168 | tf_op jit(solution)/shard_map/all_gather | solution.py:69
  56.3 0.7 iota_compare_fusion
  57.1 1.7 select_reduce_fusion.2
  58.8 4.9 %select_reduce_fusion = (f32[4,2,128]{2,1,0:T(2,128)S(1)}, f32[4,2,128,1024]{3,2,1,0:T(8,128)S(1)}) fusion(pred[4,1024]{1,0:T(4,128)(4,1)S(1)} %iota_compare_fusion, bf16[4,1024,576]{1,2,0:T(8,128)(2,1)} %param.7, bf16[2,4,128,576]{2,3,1,0:T(8,128)(2,1)} %param.9), kind=kOutput, calls=%fused_computation.7 | convolution fusion | flops 1211104256 | bytes 10100736 | tf_op jit(solution)/shard_map/vmap(shl,cl->shc)/dot_general | solution.py:16
  65.1 1.0 fusion.5
  66.2 1.6 fusion.2
  68.5 1.2 select_reduce_fusion.3
  69.6 31.2 %all-gather.6.cloned.1.call-done = bf16[16,256,576]{1,2,0:T(8,128)(2,1)} async-done(((bf16[1,256,576]{1,2,0:T(8,128)(2,1)}), bf16[16,256,576]{1,2,0:T(8,128)(2,1)}) %all-gather.6.cloned.1.call-update) | async-done | bytes 4718608 | tf_op jit(solution)/shard_map/all_gather | solution.py:67
  100.8 1.4 select_reduce_fusion.1
  102.6 1.0 dynamic-slice_bitcast_fusion
  104.3 1.3 copy.39
  105.7 25.3 %all_to_all.18 = bf16[2,5,128,512]{3,0,1,2:T(2,128)(2,1)S(1)} all-to-all(bf16[2,5,128,512]{3,0,1,2:T(2,128)(2,1)S(1)} %copy.39), channel_id=1, replica_groups=mesh['dp'=16,'tp'=16] {'tp'}, dimensions={2} | all-to-all | bytes 2621440 | tf_op jit(solution)/shard_map/all_to_all | solution.py:85
  131.3 1.0 fusion.21
  132.5 0.8 copy.80
  133.4 40.3 %all-gather.8.cloned.1.call-done = bf16[2560,1024]{1,0:T(8,128)(2,1)} async-done(((bf16[160,1024]{1,0:T(8,128)(2,1)}), bf16[2560,1024]{1,0:T(8,128)(2,1)}) %all-gather.8.cloned.1.call-update) | async-done | bytes 5242896 | tf_op jit(solution)/shard_map/all_gather | solution.py:93
  173.7 6.7 %convolution_convert_fusion = bf16[2560,448]{1,0:T(8,128)(2,1)} fusion(bf16[2560,1024]{1,0:T(8,128)(2,1)} %all-gather.8.cloned.1.call-done, bf16[1024,448]{0,1:T(8,128)(2,1)S(1)} %copy-done.1), kind=kOutput, calls=%fused_computation.2 | convolution fusion | flops 2349957120 | bytes 8454144 | tf_op jit(solution)/shard_map/dot_general | solution.py:95
  180.4 77.0 %reduce-scatter.2.cloned.1.call-done = bf16[160,448]{1,0:T(8,128)(2,1)} async-done(((bf16[2560,448]{1,0:T(8,128)(2,1)}), bf16[160,448]{1,0:T(8,128)(2,1)}) %reduce-scatter.2.cloned.1.call-update) | async-done | bytes 143376 | tf_op jit(solution)/shard_map/reduce_scatter | solution.py:94
  (45 shorter events, 7.3 us)
Async XLA Ops:
  6.5 124.8 %copy-start = (bf16[8,512,128]{2,1,0:T(8,128)(2,1)S(1)}, bf16[8,512,128]{2,1,0:T(8,128)(2,1)}, u32[]{:S(2)}) copy-start(bf16[8,512,128]{2,1,0:T(8,128)(2,1)} %param.12) | copy-start | bytes 3145732
  6.5 61.9 %all-gather.10.cloned.1.call-start = ((), (), s32[]{:S(2)}) async-start(), calls=%async_computation.5 | async-start | bytes 5013504 | tf_op jit(solution)/shard_map/all_gather | solution.py:68
  10.3 90.6 %all-gather.6.cloned.1.call-start = ((), (), s32[]{:S(2)}) async-start(), calls=%async_computation.2 | async-start | bytes 5013504 | tf_op jit(solution)/shard_map/all_gather | solution.py:67
  12.1 161.6 %all-gather.8.cloned.1.call-start = ((), (), s32[]{:S(2)}) async-start(), calls=%async_computation.3 | async-start | bytes 5570560 | tf_op jit(solution)/shard_map/all_gather | solution.py:93
  57.1 9.1 %slice-start = ((s8[4718592]{0:T(1024)(128)(4,1)}), s8[4194304]{0:T(1024)(128)(4,1)S(1)}, s32[]{:S(2)}) async-start(s8[4718592]{0:T(1024)(128)(4,1)} %bitcast.90), calls=%async_computation.6 | async-start | bytes 8388608
  58.8 7.4 %slice-start.1 = ((s8[4718592]{0:T(1024)(128)(4,1)}), s8[524288]{0:T(1024)(128)(4,1)S(1)}, s32[]{:S(2)}) async-start(s8[4718592]{0:T(1024)(128)(4,1)} %bitcast.90), calls=%async_computation.7 | async-start | bytes 1048576
  131.2 42.4 %copy-start.1 = (bf16[1024,448]{0,1:T(8,128)(2,1)S(1)}, bf16[1024,448]{0,1:T(8,128)(2,1)}, u32[]{:S(2)}) copy-start(bf16[1024,448]{0,1:T(8,128)(2,1)} %param.13) | copy-start | bytes 2752516
  133.3 124.1 %reduce-scatter.2.cloned.1.call-start = ((), (), s32[]{:S(2)}) async-start(), calls=%async_computation.4 | async-start | bytes 2785280 | tf_op jit(solution)/shard_map/reduce_scatter | solution.py:94
Sparse Core Ops, SparseCore 0:
  10.4 47.5 all-gather.9
  59.8 40.9 all-gather.5
  133.4 40.1 all-gather.7
  180.5 76.8 reduce-scatter.1
where the time goes:
time: 265 us; the launch traced here: 264 us
  waiting for transfers between devices  149 us (56%)
  blocking collectives  58.5 us (22%)
  matrix products  19.7 us (7%)
  between operations  18 us (7%)
  local copies, waits for them, and re-layouts  13.9 us (5%)
  other arithmetic  5.11 us (2%)
    reduce_scatter x1, waiting for transfers between devices, shards(): lax.psum_scatter(jnp.dot(gathered, output_weight, preferred_element_type=...  77 us
    all_gather x1, waiting for transfers between devices, shards(): gathered = lax.all_gather(flattened, 'dp', axis=0, tiled=True)  40.3 us
    all_gather x1, waiting for transfers between devices, shards(): lax.all_gather(sent_cache[None], 'dp', axis=0, tiled=True)  31.2 us
    all_to_all x1, blocking collectives, shards(): lax.all_to_all(slot_rows, 'tp', split_axis=2, concat_axis=1, tiled=True)  25.3 us
    all_gather x1, blocking collectives, shards(): lax.all_gather(sent_new[None], 'dp', axis=0, tiled=True)  18.4 us
    unnamed x1, blocking collectives  14.8 us
    dot_general x1, matrix products, shards(): jnp.dot(gathered, output_weight, preferred_element_type=jnp.float32)  6.72 us
    dot_general x2, matrix products, attend_one(): jnp.einsum('shl,cl->shc', request_query, request_cache, preferred_element...  6.28 us
  transfers between devices with their start and end apart: 4, of which 3 were waited for; matrix products, arithmetic and copies ran while one was open for 8% of the time, Pallas kernels for 0%

commit v1 on v0

v1 whole, which is shorter than its diff:
```python
import math

import jax
import jax.numpy as jnp
from jax import lax
from jax.experimental import pallas as pl
from jax.experimental.pallas import tpu as pltpu
from jax.sharding import PartitionSpec as P

NOPE = 128
ROPE = 64
VAL = 512
HEAD = 128
REQ = 4
STEPS = 2
N = 16
GROUP = 8
HOME = N * REQ * STEPS
OUT = HOME + N * STEPS
META = 16
F32 = jnp.float32
BF16 = jnp.bfloat16
SCALE = 1.0 / math.sqrt(NOPE + ROPE) * math.log2(math.e)


def attend_kernel(lengths, moves, query, cache, new, out):
    k = pl.program_id(0)

    @pl.when(k < REQ)
    def _():
        rows = STEPS * N * GROUP
        q = query[...].reshape(rows, cache.shape[2])
        keys = cache[0]
        own = new[0]
        dims = (((1,), (1,)), ((), ()))
        far = lax.dot_general(q, keys, dims, preferred_element_type=F32)
        near = lax.dot_general(q, own, dims, preferred_element_type=F32)
        filled = lengths[jnp.minimum(k, REQ - 1)]
        far_ok = lax.broadcasted_iota(jnp.int32, (1, keys.shape[0]), 1) < filled
        step = lax.broadcasted_iota(jnp.int32, near.shape, 0) // (N * GROUP)
        near_ok = lax.broadcasted_iota(jnp.int32, near.shape, 1) <= step
        far = jnp.where(far_ok, far, -jnp.inf)
        near = jnp.where(near_ok, near, -jnp.inf)
        top = jnp.maximum(
            jnp.max(far, axis=1, keepdims=True), jnp.max(near, axis=1, keepdims=True)
        )
        far = jnp.exp2((far - top) * SCALE)
        near = jnp.exp2((near - top) * SCALE)
        total = jnp.sum(far, axis=1, keepdims=True) + jnp.sum(near, axis=1, keepdims=True)
        mixed = jnp.dot(far.astype(BF16), keys[:, :VAL], preferred_element_type=F32)
        mixed = mixed + jnp.dot(near.astype(BF16), own[:, :VAL], preferred_element_type=F32)
        mixed = mixed / total
        half = N * GROUP
        out[...] = jnp.concatenate(
            [mixed[:half].reshape(N, GROUP, VAL), mixed[half:].reshape(N, GROUP, VAL)], axis=1
        ).astype(BF16)

    @pl.when(k == REQ)
    def _():
        lane = lax.broadcasted_iota(jnp.int32, out.shape, 2)
        out[...] = jnp.where(lane < 128, moves[0, 1], moves[0, 0]).astype(F32).astype(BF16)


def attend(lengths, moves, queries, cache, new):
    width = cache.shape[2]
    last = REQ - 1
    return pl.pallas_call(
        attend_kernel,
        grid_spec=pltpu.PrefetchScalarGridSpec(
            num_scalar_prefetch=2,
            grid=(REQ + 1,),
            in_specs=[
                pl.BlockSpec(
                    (STEPS, 1, N * GROUP, width), lambda k, *_: (0, jnp.minimum(k, last), 0, 0)
                ),
                pl.BlockSpec(
                    (1, cache.shape[1], width), lambda k, *_: (jnp.minimum(k, last), 0, 0)
                ),
                pl.BlockSpec((1, META, width), lambda k, *_: (jnp.minimum(k, last), 0, 0)),
            ],
            out_specs=pl.BlockSpec((N, STEPS * GROUP, VAL), lambda k, *_: (0, k, 0)),
        ),
        out_shape=jax.ShapeDtypeStruct((N, (REQ + 1) * STEPS * GROUP, VAL), BF16),
        compiler_params=pltpu.CompilerParams(vmem_limit_bytes=48 * 2**20),
    )(lengths, moves, queries, cache, new)


def value_kernel(mine, got, weight, out, wide):
    body = REQ * STEPS * GROUP
    pieces = VAL // 128
    for p in range(pieces):
        wide[p] = got[:, :body, p * 128 : (p + 1) * 128].astype(F32).reshape(N * body, 128)
    for h in range(GROUP):
        rows = jnp.concatenate(
            [wide[p, pl.ds(h, HOME, stride=GROUP), :] for p in range(pieces)], axis=1
        ).astype(BF16)
        out[:HOME, h * HEAD : (h + 1) * HEAD] = jnp.dot(
            rows, weight[h], preferred_element_type=F32
        ).astype(BF16)
    lane = lax.broadcasted_iota(jnp.int32, (N, 256), 1)
    moves = got[:, body : body + META, :256].astype(F32)[:, 0, :]
    ours = (lane % 128) // (REQ * STEPS) == mine[0]
    out[HOME:, :] = jnp.zeros((META, out.shape[1]), BF16)
    out[HOME:, :256] = jnp.where(ours, moves, 0.0).astype(BF16)


def values(mine, got, weight):
    return pl.pallas_call(
        value_kernel,
        in_specs=[
            pl.BlockSpec(memory_space=pltpu.SMEM),
            pl.BlockSpec(memory_space=pltpu.VMEM),
            pl.BlockSpec(memory_space=pltpu.VMEM),
        ],
        out_specs=pl.BlockSpec(memory_space=pltpu.VMEM),
        out_shape=jax.ShapeDtypeStruct((HOME + META, GROUP * HEAD), BF16),
        scratch_shapes=[pltpu.VMEM((VAL // 128, N * REQ * STEPS * GROUP, 128), F32)],
        compiler_params=pltpu.CompilerParams(vmem_limit_bytes=48 * 2**20),
    )(mine, got, weight)


def project_kernel(order, *refs):
    blocks, weight, out, held = refs[:N], refs[N], refs[N + 1], refs[N + 2]
    cell = REQ * STEPS
    table = jnp.zeros((N, 256), F32)
    for b in range(N):
        part = jnp.dot(blocks[b][:HOME, :], weight[...], preferred_element_type=F32)
        row = pl.multiple_of(order[b] * cell, cell)
        held[:, pl.ds(row, cell), :] = part.reshape(N, cell, part.shape[1])
        table = table + blocks[b][HOME:, :256].astype(F32)
    table = table.astype(jnp.int32)
    wide = (HOME, HOME)
    r = lax.broadcasted_iota(jnp.int32, wide, 0)
    c = lax.broadcasted_iota(jnp.int32, wide, 1)
    slot_c = (c % cell) // STEPS
    same_step = r % STEPS == c % STEPS
    per = 4
    arriving = None
    kept = None
    for j in range(N):
        rows = held[j].astype(BF16)
        target = table[j : j + 1, :HOME]
        slot = table[j : j + 1, HOME : 2 * HOME]
        moved = slot_c == slot
        keep = ((r == c) & ~moved).astype(F32).astype(BF16)
        here = (r // cell == target) & moved & same_step & ((r % cell) // STEPS == j % per)
        mine = jnp.dot(keep, rows, preferred_element_type=F32).reshape(N, cell, -1)
        came = jnp.dot(here.astype(F32).astype(BF16), rows, preferred_element_type=F32)
        arriving = came if j % per == 0 else arriving + came
        if j % 2 == 0:
            kept = mine
        else:
            out[:, (j - 1) * cell : (j + 1) * cell, :] = jnp.concatenate([kept, mine], axis=1).astype(BF16)
        if j % (2 * per) == per - 1:
            first = arriving
        if j % (2 * per) == 2 * per - 1:
            both = jnp.concatenate(
                [first.reshape(N, cell, -1), arriving.reshape(N, cell, -1)], axis=1
            )
            at = HOME + (j // (2 * per)) * 2 * cell
            out[:, at : at + 2 * cell, :] = both.astype(BF16)


def project(order, blocks, weight):
    cols = weight.shape[1]
    vmem = pl.BlockSpec(memory_space=pltpu.VMEM)
    return pl.pallas_call(
        project_kernel,
        in_specs=[pl.BlockSpec(memory_space=pltpu.SMEM)] + [vmem] * (N + 1),
        out_specs=vmem,
        out_shape=jax.ShapeDtypeStruct((N, OUT, cols), BF16),
        scratch_shapes=[pltpu.VMEM((N, HOME, cols), F32)],
        compiler_params=pltpu.CompilerParams(vmem_limit_bytes=48 * 2**20),
    )(order, *blocks, weight)


def finish_kernel(got, out):
    total = got[0].astype(F32)
    for j in range(1, N):
        total = total + got[j].astype(F32)
    rows = total.astype(BF16)
    o = lax.broadcasted_iota(jnp.int32, (OUT, OUT), 0)
    c = lax.broadcasted_iota(jnp.int32, (OUT, OUT), 1)
    slots = REQ + 1
    step, j, slot = o // (N * slots), (o // slots) % N, o % slots
    source = jnp.where(
        slot < REQ, j * (REQ * STEPS) + slot * STEPS + step, HOME + j * STEPS + step
    )
    pick = (c == source).astype(F32).astype(BF16)
    out[...] = jnp.dot(pick, rows, preferred_element_type=F32).astype(BF16)


def finish(got):
    return pl.pallas_call(
        finish_kernel,
        in_specs=[pl.BlockSpec(memory_space=pltpu.VMEM)],
        out_specs=pl.BlockSpec(memory_space=pltpu.VMEM),
        out_shape=jax.ShapeDtypeStruct(got.shape[1:], BF16),
        compiler_params=pltpu.CompilerParams(vmem_limit_bytes=48 * 2**20),
    )(got)


def along_z(by):
    chips = N // 2
    return [(z * 2 + c, (z + by) % chips * 2 + c) for z in range(chips) for c in range(2)]


OTHER_CORE = [(i, i ^ 1) for i in range(N)]


def gather(block):
    me = lax.axis_index("dp")
    chips = N // 2
    held = [(block, me)]
    up = down = block
    for hop in range(1, chips // 2 + 1):
        up = lax.ppermute(up, "dp", along_z(1))
        held.append((up, (me + N - 2 * hop) % N))
        if hop < chips // 2:
            down = lax.ppermute(down, "dp", along_z(-1))
            held.append((down, (me + 2 * hop) % N))
    held += [(lax.ppermute(b, "dp", OTHER_CORE), i ^ 1) for b, i in held]
    return [b for b, _ in held], jnp.stack([i for _, i in held]).astype(jnp.int32)


def shards(latent_cache, lengths, queries, new_latents, migrations, value_weight, output_weight):
    leaving = migrations[:, 0] < REQ
    moves = jnp.stack([migrations[:, 0], jnp.where(leaving, migrations[:, 1], -1)], axis=1)
    new = jnp.pad(jnp.swapaxes(new_latents, 0, 1), ((0, 0), (0, META - STEPS), (0, 0)))
    sent = attend(lengths, moves, queries, latent_cache, new)
    got = lax.all_to_all(sent, "tp", split_axis=0, concat_axis=0, tiled=True)
    me = lax.axis_index("dp").astype(jnp.int32).reshape(1)
    hidden = values(me, got, value_weight)
    blocks, order = gather(hidden)
    partial = project(order, blocks, output_weight)
    shares = lax.all_to_all(partial, "tp", split_axis=0, concat_axis=0, tiled=True)
    return finish(shares)


def solution(mesh):
    return jax.shard_map(
        shards,
        mesh=mesh,
        in_specs=(
            P(("dp", "tp"), None, None),
            P(("dp", "tp")),
            P(None, ("dp", "tp"), None, None),
            P(None, ("dp", "tp"), None),
            P(("dp", "tp"), None),
            P("tp", None, None),
            P("tp", "dp"),
        ),
        out_specs=P("tp", "dp"),
        check_vma=False,
    )
```

time: 265 us -> 138 us (0.52)
  waiting for transfers between devices: 149 us -> 26.4 us
  starting transfers between devices: 0.13 us -> 38.4 us
  blocking collectives: 58.5 us -> 36.3 us
  matrix products: 19.7 us -> 0 us
  Pallas kernels: 0 us -> 19.1 us
  between operations: 18 us -> 1.49 us
  other arithmetic: 5.11 us -> 0.76 us
    reduce_scatter x1 -> x0, waiting for transfers between devices: 77 us -> none  [shards(): lax.psum_scatter(jnp.dot(gathered, output_weight, preferred_element_type=...]
    all_gather x3 -> x0, waiting for transfers between devices: 71.5 us -> none  [the longest x1 40.3 us: shards(): gathered = lax.all_gather(flattened, 'dp', axis=0, tiled=True)]
    ppermute x0 -> x15, starting transfers between devices: none -> 30.7 us  [the longest x8 19.1 us: gather(): held += [(lax.ppermute(b, 'dp', OTHER_CORE), i ^ 1) for b, i in held]]
    dot_general x10 -> x0, matrix products: 19.7 us -> none  [the longest x1 6.72 us: shards(): jnp.dot(gathered, output_weight, preferred_element_type=jnp.float32)]
    pallas_call x0 -> x4, Pallas kernels: none -> 19.1 us  [the longest x1 10.5 us: attend(): pl.pallas_call(attend_kernel, grid_spec=pltpu.PrefetchScalarGridSpec(num_...]
    all_gather x1 -> x0, blocking collectives: 18.4 us -> none  [shards(): lax.all_gather(sent_new[None], 'dp', axis=0, tiled=True)]
    all_to_all x0 -> x1, waiting for transfers between devices: none -> 18.1 us  [shards(): got = lax.all_to_all(sent, 'tp', split_axis=0, concat_axis=0, tiled=True)]
    unnamed x1 -> x0, blocking collectives: 14.8 us -> none
  transfers between devices with their start and end apart: 4 -> 16, of which waited for: 3 -> 3; matrix products, arithmetic and copies ran while one was open for 8% -> 1% of each run, Pallas kernels for 0% -> 0%
where the time goes in v1:
time: 138 us; the launch traced here: 137 us
  starting transfers between devices  38.4 us (28%)
  blocking collectives  36.3 us (26%)
  waiting for transfers between devices  26.4 us (19%)
  Pallas kernels  19.1 us (14%)
  local copies, waits for them, and re-layouts  14.8 us (11%)
  between operations  1.49 us (1%)
    all_to_all x1, blocking collectives, shards(): lax.all_to_all(partial, 'tp', split_axis=0, concat_axis=0, tiled=True)  36.3 us
    ppermute x8, starting transfers between devices, gather(): held += [(lax.ppermute(b, 'dp', OTHER_CORE), i ^ 1) for b, i in held]  19.1 us
    all_to_all x1, waiting for transfers between devices, shards(): got = lax.all_to_all(sent, 'tp', split_axis=0, concat_axis=0, tiled=True)  18.1 us
    unnamed x20, local copies, waits for them, and re-layouts  13.3 us
    pallas_call x1, Pallas kernels, attend(): pl.pallas_call(attend_kernel, grid_spec=pltpu.PrefetchScalarGridSpec(num_...  10.5 us
    ppermute x3, starting transfers between devices, gather(): down = lax.ppermute(down, 'dp', along_z(-1))  9.9 us
    ppermute x4, waiting for transfers between devices, gather(): up = lax.ppermute(up, 'dp', along_z(1))  8.28 us
    all_to_all x1, starting transfers between devices, shards(): got = lax.all_to_all(sent, 'tp', split_axis=0, concat_axis=0, tiled=True)  7.72 us
  transfers between devices with their start and end apart: 16, of which 3 were waited for; matrix products, arithmetic and copies ran while one was open for 1% of the time, Pallas kernels for 0%

profile of v1, /device:TPU:1, one launch (start us, length us, event | category | flops | bytes accessed | tf_op | source)
XLA Modules:
  0.0 137.2 jit_solution(18332778313014675766)
XLA Ops:
  0.0 1.3 fusion
  2.7 0.8 pad_add_fusion.moves
  3.4 7.8 %copy.10.cache = bf16[4,1024,576]{2,1,0:T(8,128)(2,1)} copy(bf16[4,1024,576]{1,2,0:T(8,128)(2,1)} %param.7) | data formatting | bytes 9437184 | tf_op args[0]
  12.0 10.5 %shard_map.73 = bf16[16,80,512]{2,1,0:T(8,128)(2,1)} custom-call(s32[4]{0:T(128)S(1)} %copy-done.5, s32[1,2]{1,0:T(1,128)S(1)} %pad_add_fusion.moves, bf16[2,4,128,576]{3,2,1,0:T(8,128)(2,1)S(1)} %copy.9.query, bf16[4,1024,576]{2,1,0:T(8,128)(2,1)} %copy.10.cache, bf16[4,16,576]{2,1,0:T(8,128)(2,1)S(1)} %pad.4.new), custom_call_target="tpu_custom_call" | custom-call | tf_op jit(solution)/shard_map/pallas_call | solution.py:67
  22.5 7.7 %all-to-all-start = ((bf16[16,80,512]{2,1,0:T(8,128)(2,1)}), bf16[16,80,512]{2,1,0:T(8,128)(2,1)S(1)}, u32[]{:S(2)}, u32[]{:S(2)}) async-start(bf16[16,80,512]{2,1,0:T(8,128)(2,1)} %shard_map.73), calls=%async_computation | async-start | bytes 2621440 | tf_op jit(solution)/shard_map/all_to_all | solution.py:231
  30.2 18.1 %all-to-all-done.got = bf16[16,80,512]{2,1,0:T(8,128)(2,1)S(1)} async-done(((bf16[16,80,512]{2,1,0:T(8,128)(2,1)}), bf16[16,80,512]{2,1,0:T(8,128)(2,1)S(1)}, u32[]{:S(2)}, u32[]{:S(2)}) %all-to-all-start) | async-done | bytes 1310752 | tf_op jit(solution)/shard_map/all_to_all | solution.py:231
  48.3 0.8 shard_map.74.refs_0_
  49.1 1.7 %collective-permute-start = (bf16[144,1024]{1,0:T(8,128)(2,1)S(1)}, bf16[144,1024]{1,0:T(8,128)(2,1)S(1)}, u32[]{:S(2)}, u32[]{:S(2)}) collective-permute-start(bf16[144,1024]{1,0:T(8,128)(2,1)S(1)} %shard_map.74.refs_0_), channel_id=1, source_target_pairs={{0,32},{16,48},{32,64},{48,80},{64,96},{80,112},{96,128},{112,144}... | collective-permute-start | bytes 884744 | tf_op jit(solution)/shard_map/ppermute | solution.py:217
  50.8 4.0 %collective-permute-start.1 = (bf16[144,1024]{1,0:T(8,128)(2,1)S(1)}, bf16[144,1024]{1,0:T(8,128)(2,1)S(1)}, u32[]{:S(2)}, u32[]{:S(2)}) collective-permute-start(bf16[144,1024]{1,0:T(8,128)(2,1)S(1)} %shard_map.74.refs_0_), channel_id=1, source_target_pairs={{0,224},{16,240},{32,0},{48,16},{64,32},{80,48},{96,64},{112,80},{... | collective-permute-start | bytes 884744 | tf_op jit(solution)/shard_map/ppermute | solution.py:220
  54.8 4.0 %collective-permute-done.refs_1_ = bf16[144,1024]{1,0:T(8,128)(2,1)S(1)} collective-permute-done((bf16[144,1024]{1,0:T(8,128)(2,1)S(1)}, bf16[144,1024]{1,0:T(8,128)(2,1)S(1)}, u32[]{:S(2)}, u32[]{:S(2)}) %collective-permute-start) | collective-permute-done | bytes 294944 | tf_op jit(solution)/shard_map/ppermute | solution.py:217
  58.8 2.8 %collective-permute-start.3 = (bf16[144,1024]{1,0:T(8,128)(2,1)S(1)}, bf16[144,1024]{1,0:T(8,128)(2,1)S(1)}, u32[]{:S(2)}, u32[]{:S(2)}) collective-permute-start(bf16[144,1024]{1,0:T(8,128)(2,1)S(1)} %collective-permute-done.1.refs_2_), channel_id=1, source_target_pairs={{0,224},{16,240},{32,0},{48,16},{64,32},{80,48},{96,64},{112,80},{... | collective-permute-start | bytes 884744 | tf_op jit(solution)/shard_map/ppermute | solution.py:220
  61.6 4.3 %collective-permute-done.2.refs_3_ = bf16[144,1024]{1,0:T(8,128)(2,1)S(1)} collective-permute-done((bf16[144,1024]{1,0:T(8,128)(2,1)S(1)}, bf16[144,1024]{1,0:T(8,128)(2,1)S(1)}, u32[]{:S(2)}, u32[]{:S(2)}) %collective-permute-start.2) | collective-permute-done | bytes 294944 | tf_op jit(solution)/shard_map/ppermute | solution.py:217
  65.8 7.4 %collective-permute-start.7 = (bf16[144,1024]{1,0:T(8,128)(2,1)S(1)}, bf16[144,1024]{1,0:T(8,128)(2,1)S(1)}, u32[]{:S(2)}, u32[]{:S(2)}) collective-permute-start(bf16[144,1024]{1,0:T(8,128)(2,1)S(1)} %shard_map.74.refs_0_), channel_id=1, source_target_pairs={{0,16},{16,0},{32,48},{48,32},{64,80},{80,64},{96,112},{112,96},{1... | collective-permute-start | bytes 884744 | tf_op jit(solution)/shard_map/ppermute | solution.py:222
  73.8 3.1 %collective-permute-start.5 = (bf16[144,1024]{1,0:T(8,128)(2,1)S(1)}, bf16[144,1024]{1,0:T(8,128)(2,1)}, u32[]{:S(2)}, u32[]{:S(2)}) collective-permute-start(bf16[144,1024]{1,0:T(8,128)(2,1)S(1)} %collective-permute-done.3.refs_4_), channel_id=1, source_target_pairs={{0,224},{16,240},{32,0},{48,16},{64,32},{80,48},{96,64},{112,80},{... | collective-permute-start | bytes 884744 | tf_op jit(solution)/shard_map/ppermute | solution.py:220
  76.9 4.5 %collective-permute-start.10 = (bf16[144,1024]{1,0:T(8,128)(2,1)S(1)}, bf16[144,1024]{1,0:T(8,128)(2,1)}, u32[]{:S(2)}, u32[]{:S(2)}) collective-permute-start(bf16[144,1024]{1,0:T(8,128)(2,1)S(1)} %collective-permute-done.2.refs_3_), channel_id=1, source_target_pairs={{0,16},{16,0},{32,48},{48,32},{64,80},{80,64},{96,112},{112,96},{1... | collective-permute-start | bytes 884744 | tf_op jit(solution)/shard_map/ppermute | solution.py:222
  82.2 0.7 copy-done.3
  83.4 0.7 collective-permute-start.13
  84.1 5.4 %collective-permute-start.14 = (bf16[144,1024]{1,0:T(8,128)(2,1)}, bf16[144,1024]{1,0:T(8,128)(2,1)}, u32[]{:S(2)}, u32[]{:S(2)}) collective-permute-start(bf16[144,1024]{1,0:T(8,128)(2,1)} %collective-permute-done.6.refs_7_), channel_id=1, source_target_pairs={{0,16},{16,0},{32,48},{48,32},{64,80},{80,64},{96,112},{112,96},{1... | collective-permute-start | bytes 884744 | tf_op jit(solution)/shard_map/ppermute | solution.py:222
  89.5 1.5 %copy.11.refs_16_ = bf16[1024,448]{1,0:T(8,128)(2,1)S(1)} copy(bf16[1024,448]{0,1:T(8,128)(2,1)} %param.13) | data formatting | bytes 1835008 | tf_op args[6]
  91.1 1.0 copy-done.2
  92.1 1.0 copy-done.4
  93.0 6.6 %shard_map.75 = bf16[16,160,448]{2,1,0:T(8,128)(2,1)} custom-call(s32[16]{0:T(128)S(1)} %stack.71.order, bf16[144,1024]{1,0:T(8,128)(2,1)S(1)} %shard_map.74.refs_0_, bf16[144,1024]{1,0:T(8,128)(2,1)S(1)} %collective-permute-done.refs_1_, bf16[144,1024]{1,0:T(8,128)(2,1)S(1)} %collective-permute-done.1.refs_2_, ...), custom_call_target="tpu_custom_call" | custom-call | tf_op jit(solution)/shard_map/pallas_call | solution.py:167
  99.6 36.3 %all_to_all.10.got = bf16[16,160,448]{2,1,0:T(8,128)(2,1)S(1)} all-to-all(bf16[16,160,448]{2,1,0:T(8,128)(2,1)} %shard_map.75), channel_id=1, replica_groups=mesh['dp'=16,'tp'=16] {'tp'}, dimensions={0} | all-to-all | bytes 4587520 | tf_op jit(solution)/shard_map/all_to_all | solution.py:236
  135.9 1.2 shard_map.76
  (37 shorter events, 2.6 us)
Async XLA Ops:
  3.4 7.8 %copy-start.6 = (bf16[2,4,128,576]{2,3,1,0:T(8,128)(2,1)S(1)}, bf16[2,4,128,576]{2,3,1,0:T(8,128)(2,1)}, u32[]{:S(2)}) copy-start(bf16[2,4,128,576]{2,3,1,0:T(8,128)(2,1)} %param.9) | copy-start | bytes 3538948
  3.4 8.5 %copy-start.7 = (bf16[2,4,576]{2,1,0:T(4,128)(2,1)S(1)}, bf16[2,4,576]{2,1,0:T(4,128)(2,1)}, u32[]{:S(2)}) copy-start(bf16[2,4,576]{2,1,0:T(4,128)(2,1)} %param.10) | copy-start | bytes 27652
  3.4 8.6 %copy-start.5 = (s32[4]{0:T(128)S(1)}, s32[4]{0:T(128)}, u32[]{:S(2)}) copy-start(s32[4]{0:T(128)} %lengths.1) | copy-start | bytes 52
  22.5 25.8 %copy-start = (bf16[8,512,128]{2,1,0:T(8,128)(2,1)S(1)}, bf16[8,512,128]{2,1,0:T(8,128)(2,1)}, u32[]{:S(2)}) copy-start(bf16[8,512,128]{2,1,0:T(8,128)(2,1)} %weight.1) | copy-start | bytes 3145732
  22.5 25.8 %all-to-all-start = ((bf16[16,80,512]{2,1,0:T(8,128)(2,1)}), bf16[16,80,512]{2,1,0:T(8,128)(2,1)S(1)}, u32[]{:S(2)}, u32[]{:S(2)}) async-start(bf16[16,80,512]{2,1,0:T(8,128)(2,1)} %shard_map.73), calls=%async_computation | async-start | bytes 2621440 | tf_op jit(solution)/shard_map/all_to_all | solution.py:231
  49.1 9.8 %collective-permute-start = (bf16[144,1024]{1,0:T(8,128)(2,1)S(1)}, bf16[144,1024]{1,0:T(8,128)(2,1)S(1)}, u32[]{:S(2)}, u32[]{:S(2)}) collective-permute-start(bf16[144,1024]{1,0:T(8,128)(2,1)S(1)} %shard_map.74.refs_0_), channel_id=1, source_target_pairs={{0,32},{16,48},{32,64},{48,80},{64,96},{80,112},{96,128},{112,144}... | collective-permute-start | bytes 884744 | tf_op jit(solution)/shard_map/ppermute | solution.py:217
  50.8 8.1 %collective-permute-start.1 = (bf16[144,1024]{1,0:T(8,128)(2,1)S(1)}, bf16[144,1024]{1,0:T(8,128)(2,1)S(1)}, u32[]{:S(2)}, u32[]{:S(2)}) collective-permute-start(bf16[144,1024]{1,0:T(8,128)(2,1)S(1)} %shard_map.74.refs_0_), channel_id=1, source_target_pairs={{0,224},{16,240},{32,0},{48,16},{64,32},{80,48},{96,64},{112,80},{... | collective-permute-start | bytes 884744 | tf_op jit(solution)/shard_map/ppermute | solution.py:220
  58.8 7.0 %collective-permute-start.2 = (bf16[144,1024]{1,0:T(8,128)(2,1)S(1)}, bf16[144,1024]{1,0:T(8,128)(2,1)S(1)}, u32[]{:S(2)}, u32[]{:S(2)}) collective-permute-start(bf16[144,1024]{1,0:T(8,128)(2,1)S(1)} %collective-permute-done.refs_1_), channel_id=1, source_target_pairs={{0,32},{16,48},{32,64},{48,80},{64,96},{80,112},{96,128},{112,144}... | collective-permute-start | bytes 884744 | tf_op jit(solution)/shard_map/ppermute | solution.py:217
  58.8 15.0 %collective-permute-start.3 = (bf16[144,1024]{1,0:T(8,128)(2,1)S(1)}, bf16[144,1024]{1,0:T(8,128)(2,1)S(1)}, u32[]{:S(2)}, u32[]{:S(2)}) collective-permute-start(bf16[144,1024]{1,0:T(8,128)(2,1)S(1)} %collective-permute-done.1.refs_2_), channel_id=1, source_target_pairs={{0,224},{16,240},{32,0},{48,16},{64,32},{80,48},{96,64},{112,80},{... | collective-permute-start | bytes 884744 | tf_op jit(solution)/shard_map/ppermute | solution.py:220
  65.8 11.1 %collective-permute-start.4 = (bf16[144,1024]{1,0:T(8,128)(2,1)S(1)}, bf16[144,1024]{1,0:T(8,128)(2,1)S(1)}, u32[]{:S(2)}, u32[]{:S(2)}) collective-permute-start(bf16[144,1024]{1,0:T(8,128)(2,1)S(1)} %collective-permute-done.2.refs_3_), channel_id=1, source_target_pairs={{0,32},{16,48},{32,64},{48,80},{64,96},{80,112},{96,128},{112,144}... | collective-permute-start | bytes 884744 | tf_op jit(solution)/shard_map/ppermute | solution.py:217
  65.8 11.1 %collective-permute-start.7 = (bf16[144,1024]{1,0:T(8,128)(2,1)S(1)}, bf16[144,1024]{1,0:T(8,128)(2,1)S(1)}, u32[]{:S(2)}, u32[]{:S(2)}) collective-permute-start(bf16[144,1024]{1,0:T(8,128)(2,1)S(1)} %shard_map.74.refs_0_), channel_id=1, source_target_pairs={{0,16},{16,0},{32,48},{48,32},{64,80},{80,64},{96,112},{112,96},{1... | collective-permute-start | bytes 884744 | tf_op jit(solution)/shard_map/ppermute | solution.py:222
  73.3 8.2 %collective-permute-start.8 = (bf16[144,1024]{1,0:T(8,128)(2,1)S(1)}, bf16[144,1024]{1,0:T(8,128)(2,1)S(1)}, u32[]{:S(2)}, u32[]{:S(2)}) collective-permute-start(bf16[144,1024]{1,0:T(8,128)(2,1)S(1)} %collective-permute-done.refs_1_), channel_id=1, source_target_pairs={{0,16},{16,0},{32,48},{48,32},{64,80},{80,64},{96,112},{112,96},{1... | collective-permute-start | bytes 884744 | tf_op jit(solution)/shard_map/ppermute | solution.py:222
  73.3 8.9 %collective-permute-start.9 = (bf16[144,1024]{1,0:T(8,128)(2,1)S(1)}, bf16[144,1024]{1,0:T(8,128)(2,1)S(1)}, u32[]{:S(2)}, u32[]{:S(2)}) collective-permute-start(bf16[144,1024]{1,0:T(8,128)(2,1)S(1)} %collective-permute-done.1.refs_2_), channel_id=1, source_target_pairs={{0,16},{16,0},{32,48},{48,32},{64,80},{80,64},{96,112},{112,96},{1... | collective-permute-start | bytes 884744 | tf_op jit(solution)/shard_map/ppermute | solution.py:222
  73.8 9.6 %collective-permute-start.5 = (bf16[144,1024]{1,0:T(8,128)(2,1)S(1)}, bf16[144,1024]{1,0:T(8,128)(2,1)}, u32[]{:S(2)}, u32[]{:S(2)}) collective-permute-start(bf16[144,1024]{1,0:T(8,128)(2,1)S(1)} %collective-permute-done.3.refs_4_), channel_id=1, source_target_pairs={{0,224},{16,240},{32,0},{48,16},{64,32},{80,48},{96,64},{112,80},{... | collective-permute-start | bytes 884744 | tf_op jit(solution)/shard_map/ppermute | solution.py:220
  76.9 7.2 %collective-permute-start.6 = (bf16[144,1024]{1,0:T(8,128)(2,1)S(1)}, bf16[144,1024]{1,0:T(8,128)(2,1)}, u32[]{:S(2)}, u32[]{:S(2)}) collective-permute-start(bf16[144,1024]{1,0:T(8,128)(2,1)S(1)} %collective-permute-done.4.refs_5_), channel_id=1, source_target_pairs={{0,32},{16,48},{32,64},{48,80},{64,96},{80,112},{96,128},{112,144}... | collective-permute-start | bytes 884744 | tf_op jit(solution)/shard_map/ppermute | solution.py:217
  76.9 14.1 %collective-permute-start.10 = (bf16[144,1024]{1,0:T(8,128)(2,1)S(1)}, bf16[144,1024]{1,0:T(8,128)(2,1)}, u32[]{:S(2)}, u32[]{:S(2)}) collective-permute-start(bf16[144,1024]{1,0:T(8,128)(2,1)S(1)} %collective-permute-done.2.refs_3_), channel_id=1, source_target_pairs={{0,16},{16,0},{32,48},{48,32},{64,80},{80,64},{96,112},{112,96},{1... | collective-permute-start | bytes 884744 | tf_op jit(solution)/shard_map/ppermute | solution.py:222
  81.5 0.7 copy-start.1
  82.2 8.9 %collective-permute-start.11 = (bf16[144,1024]{1,0:T(8,128)(2,1)S(1)}, bf16[144,1024]{1,0:T(8,128)(2,1)}, u32[]{:S(2)}, u32[]{:S(2)}) collective-permute-start(bf16[144,1024]{1,0:T(8,128)(2,1)S(1)} %collective-permute-done.3.refs_4_), channel_id=1, source_target_pairs={{0,16},{16,0},{32,48},{48,32},{64,80},{80,64},{96,112},{112,96},{1... | collective-permute-start | bytes 884744 | tf_op jit(solution)/shard_map/ppermute | solution.py:222
  82.2 0.7 copy-start.3
  82.9 8.2 %collective-permute-start.12 = (bf16[144,1024]{1,0:T(8,128)(2,1)S(1)}, bf16[144,1024]{1,0:T(8,128)(2,1)}, u32[]{:S(2)}, u32[]{:S(2)}) collective-permute-start(bf16[144,1024]{1,0:T(8,128)(2,1)S(1)} %collective-permute-done.4.refs_5_), channel_id=1, source_target_pairs={{0,16},{16,0},{32,48},{48,32},{64,80},{80,64},{96,112},{112,96},{1... | collective-permute-start | bytes 884744 | tf_op jit(solution)/shard_map/ppermute | solution.py:222
  83.4 7.7 %collective-permute-start.13 = (bf16[144,1024]{1,0:T(8,128)(2,1)}, bf16[144,1024]{1,0:T(8,128)(2,1)}, u32[]{:S(2)}, u32[]{:S(2)}) collective-permute-start(bf16[144,1024]{1,0:T(8,128)(2,1)} %collective-permute-done.5.refs_6_), channel_id=1, source_target_pairs={{0,16},{16,0},{32,48},{48,32},{64,80},{80,64},{96,112},{112,96},{1... | collective-permute-start | bytes 884744 | tf_op jit(solution)/shard_map/ppermute | solution.py:222
  84.1 7.0 %collective-permute-start.14 = (bf16[144,1024]{1,0:T(8,128)(2,1)}, bf16[144,1024]{1,0:T(8,128)(2,1)}, u32[]{:S(2)}, u32[]{:S(2)}) collective-permute-start(bf16[144,1024]{1,0:T(8,128)(2,1)} %collective-permute-done.6.refs_7_), channel_id=1, source_target_pairs={{0,16},{16,0},{32,48},{48,32},{64,80},{80,64},{96,112},{112,96},{1... | collective-permute-start | bytes 884744 | tf_op jit(solution)/shard_map/ppermute | solution.py:222
  91.1 1.0 copy-start.2
  92.1 1.0 copy-start.4

commit v2 on v0

v2 whole, which is shorter than its diff:
```python
import math

import jax
import jax.numpy as jnp
from jax import lax
from jax.experimental import pallas as pl
from jax.experimental.pallas import tpu as pltpu
from jax.sharding import PartitionSpec as P

NOPE = 128
ROPE = 64
VAL = 512
HEAD = 128
REQ = 4
STEPS = 2
N = 16
GROUP = 8
META = 16
LANES = 128
CHUNKS = ((0, 4),)
ARRIVING = N * STEPS
TOGETHER = 2
F32 = jnp.float32
BF16 = jnp.bfloat16
SCALE = 1.0 / math.sqrt(NOPE + ROPE) * math.log2(math.e)
NT = (((1,), (1,)), ((), ()))


def attend_one(q, keys, own, filled):
    far = jnp.dot(q, keys, preferred_element_type=F32)
    near = lax.dot_general(q, own, NT, preferred_element_type=F32)
    far_ok = lax.broadcasted_iota(jnp.int32, (1, keys.shape[1]), 1) < filled
    step = lax.broadcasted_iota(jnp.int32, near.shape, 0) // (N * GROUP)
    near_ok = lax.broadcasted_iota(jnp.int32, near.shape, 1) <= step
    far = jnp.where(far_ok, far, -jnp.inf)
    near = jnp.where(near_ok, near, -jnp.inf)
    top = jnp.maximum(jnp.max(far, axis=1, keepdims=True), jnp.max(near, axis=1, keepdims=True))
    far = jnp.exp2((far - top) * SCALE)
    near = jnp.exp2((near - top) * SCALE)
    total = jnp.sum(far, axis=1, keepdims=True) + jnp.sum(near, axis=1, keepdims=True)
    mixed = lax.dot_general(far.astype(BF16), keys[:VAL], NT, preferred_element_type=F32)
    mixed = mixed + jnp.dot(near.astype(BF16), own[:, :VAL], preferred_element_type=F32)
    return mixed / total


def attend_kernel(lengths, moves, query, cache, new, out):
    half = N * GROUP
    rows = STEPS * GROUP
    body = REQ * rows
    turn = pl.program_id(0)
    for u in range(TOGETHER):
        request = turn * TOGETHER + u
        q = jnp.concatenate([query[s, u].T for s in range(STEPS)], axis=0)
        fresh = new[...].astype(F32)
        fresh = jnp.where(turn == 0, fresh[:, u, :], fresh[:, TOGETHER + u, :])
        own = jnp.concatenate([fresh, jnp.zeros((META - STEPS, fresh.shape[1]), F32)], axis=0)
        mixed = attend_one(q, cache[u], own.astype(BF16), lengths[request])
        mixed = jnp.concatenate(
            [mixed[:half].reshape(N, GROUP, VAL), mixed[half:].reshape(N, GROUP, VAL)], axis=1
        ).astype(BF16)
        for p in range(VAL // LANES):
            at = pl.multiple_of(p * body + request * rows, rows)
            out[:, pl.ds(at, rows), :] = mixed[:, :, p * LANES : (p + 1) * LANES]
    lane = lax.broadcasted_iota(jnp.int32, (N, META, LANES), 2)
    slot = moves[0, 0]
    taker = jnp.where(slot < REQ, moves[0, 1], -1)
    out[:, body * (VAL // LANES) :, :] = (
        jnp.where(lane < LANES // 2, taker, slot).astype(F32).astype(BF16)
    )


def attend(lengths, moves, queries, cache, new):
    width = cache.shape[1]
    rows = REQ * STEPS * GROUP * (VAL // LANES) + META
    return pl.pallas_call(
        attend_kernel,
        grid_spec=pltpu.PrefetchScalarGridSpec(
            num_scalar_prefetch=2,
            grid=(REQ // TOGETHER,),
            in_specs=[
                pl.BlockSpec((STEPS, TOGETHER, width, N * GROUP), lambda g, *_: (0, g, 0, 0)),
                pl.BlockSpec((TOGETHER, width, cache.shape[2]), lambda g, *_: (g, 0, 0)),
                pl.BlockSpec(new.shape, lambda g, *_: (0, 0, 0)),
            ],
            out_specs=pl.BlockSpec((N, rows, LANES), lambda g, *_: (0, 0, 0)),
        ),
        out_shape=jax.ShapeDtypeStruct((N, rows, LANES), BF16),
        compiler_params=pltpu.CompilerParams(vmem_limit_bytes=56 * 2**20),
    )(lengths, moves, queries, cache, new)


def value_kernel(got, weight, *refs):
    outs, wide = refs[:-1], refs[-1]
    body = REQ * STEPS * GROUP
    pieces = VAL // LANES
    moves = got[:, pieces * body :, :].astype(F32)[:, 0, :]
    sub = lax.broadcasted_iota(jnp.int32, (N, LANES), 0)
    lane = lax.broadcasted_iota(jnp.int32, (N, LANES), 1)
    taker = jnp.max(jnp.where(lane < LANES // 2, moves, -1.0), axis=1, keepdims=True)
    slot = jnp.max(jnp.where(lane < LANES // 2, -1.0, moves), axis=1, keepdims=True)
    parts = []
    for (first, count), out in zip(CHUNKS, outs, strict=True):
        cell = count * STEPS * GROUP
        home = N * count * STEPS
        for p in range(pieces):
            at = p * body + first * STEPS * GROUP
            wide[p, : N * cell, :] = got[:, at : at + cell, :].astype(F32).reshape(N * cell, LANES)
        for h in range(GROUP):
            rows = jnp.concatenate(
                [wide[p, pl.ds(h, home, stride=GROUP), :] for p in range(pieces)], axis=1
            ).astype(BF16)
            out[h * home : (h + 1) * home, :] = jnp.dot(
                rows, weight[h], preferred_element_type=F32
            ).astype(BF16)
        mine = lane // (count * STEPS) == sub
        for v in (taker, slot):
            parts.append(jnp.sum(jnp.where(mine, v, 0.0), axis=0, keepdims=True))
    row = lax.broadcasted_iota(jnp.int32, (META, LANES), 0)
    lines = jnp.zeros((META, LANES), F32)
    for i, part in enumerate(parts):
        lines = jnp.where(row == i, part, lines)
    out[GROUP * home :, :] = lines.astype(BF16)


def values(got, weight):
    homes = [N * count * STEPS for _, count in CHUNKS]
    shapes = [(h * GROUP + (META if p == len(homes) - 1 else 0), HEAD) for p, h in enumerate(homes)]
    whole = [pl.BlockSpec(s, lambda g: (0, 0)) for s in shapes]
    return pl.pallas_call(
        value_kernel,
        grid=(1,),
        in_specs=[
            pl.BlockSpec(got.shape, lambda g: (0, 0, 0)),
            pl.BlockSpec(weight.shape, lambda g: (0, 0, 0)),
        ],
        out_specs=whole,
        out_shape=[jax.ShapeDtypeStruct(s, BF16) for s in shapes],
        scratch_shapes=[pltpu.VMEM((VAL // LANES, max(homes) * GROUP, LANES), F32)],
        compiler_params=pltpu.CompilerParams(vmem_limit_bytes=24 * 2**20),
    )(got, weight)


def pack(rows):
    full = rows.shape[2] // LANES
    half = rows.shape[1] // 2
    tail = rows[:, :, full * LANES :]
    return [rows[:, :, t * LANES : (t + 1) * LANES] for t in range(full)] + [
        jnp.concatenate([tail[:, :half], tail[:, half:]], axis=2)
    ]


def unpack(packed, count):
    half = count // 2
    full = (packed.shape[0] - half) // count
    tail = packed[full * count :]
    tail = jnp.concatenate([tail[:, : LANES // 2], tail[:, LANES // 2 :]], axis=0)
    return jnp.concatenate([packed[t * count : (t + 1) * count] for t in range(full)] + [tail], axis=1)


def put(out, parts):
    at = 0
    for part in parts:
        out[:, at : at + part.shape[1], :] = part.astype(BF16)
        at += part.shape[1]


def fetch(order, blocks, held, sem):
    copies = [
        pltpu.make_async_copy(block, held.at[order[b]], sem.at[b])
        for b, block in enumerate(blocks)
    ]
    for copy in copies:
        copy.start()
    for copy in copies:
        copy.wait()


def multiply(held, home, weight):
    rows = jnp.concatenate(
        [held[:, h * home : (h + 1) * home, :].reshape(N * home, HEAD) for h in range(GROUP)], axis=1
    )
    rows = lax.dot_general(rows, weight[...], NT, preferred_element_type=F32)
    return rows.reshape(N, home, rows.shape[1]).astype(BF16)


def project_kernel(count, order, *refs):
    blocks, (weight, out, home_out, held, sem) = refs[:-5], refs[-5:]
    fetch(order, blocks, held, sem)
    rows = multiply(held, N * count * STEPS, weight)
    put(out, pack(rows.astype(F32)))
    home_out[...] = rows


def last_kernel(counts, order, *refs):
    parts = len(counts)
    refs, (weight, out, table_out, held, sem) = refs[:-5], refs[-5:]
    cut = len(refs) - (parts - 1)
    blocks, earlier = refs[:cut], refs[cut:]
    count = counts[-1]
    home = N * count * STEPS
    fetch(order, blocks, held, sem)
    table = held[:, GROUP * home :, :].astype(F32)
    table_out[...] = table
    table = table.astype(jnp.int32)
    rows = multiply(held, home, weight)
    cols = rows.shape[2]
    came = jnp.zeros((N * ARRIVING, cols), F32)
    for p, c in enumerate(counts):
        size = N * c * STEPS
        first = sum(counts[:p])
        lane = lax.broadcasted_iota(jnp.int32, (N, size), 1)
        taker = table[:, 2 * p, :size]
        slot = table[:, 2 * p + 1, :size]
        here = slot == first + (lane // STEPS) % c
        code = jnp.where(here, (taker * N + lane // (c * STEPS)) * STEPS + lane % STEPS, -1)
        source = rows if p == parts - 1 else earlier[p][...]
        group = max(1, 256 // size)
        for e in range(0, N, group):
            wanted = jnp.concatenate([code[e + g : e + g + 1] for g in range(group)], axis=1)
            r = lax.broadcasted_iota(jnp.int32, (N * ARRIVING, group * size), 0)
            pick = (r == wanted).astype(F32).astype(BF16)
            came = came + jnp.dot(
                pick, source[e : e + group].reshape(group * size, cols), preferred_element_type=F32
            )
    both = jnp.concatenate([rows.astype(F32), came.reshape(N, ARRIVING, cols)], axis=1)
    put(out, pack(both))


def project(counts, order, blocks, weight, earlier):
    cols, depth = weight.shape
    count = counts[-1]
    home = N * count * STEPS
    last = len(counts) == len(CHUNKS)
    sent = home + (ARRIVING if last else 0)
    earlier = earlier if last else []

    def kernel(*refs):
        if last:
            last_kernel(counts, *refs)
        else:
            project_kernel(count, *refs)

    def whole(shape):
        return pl.BlockSpec(shape, lambda g, *_: (0,) * len(shape))

    shapes = [(N, sent * cols // LANES, LANES), (N, META, LANES) if last else (N, home, cols)]
    return pl.pallas_call(
        kernel,
        grid_spec=pltpu.PrefetchScalarGridSpec(
            num_scalar_prefetch=1,
            grid=(1,),
            in_specs=[pl.BlockSpec(memory_space=pltpu.HBM)] * len(blocks)
            + [whole(e.shape) for e in earlier]
            + [whole(weight.shape)],
            out_specs=[whole(s) for s in shapes],
            scratch_shapes=[
                pltpu.VMEM((N,) + blocks[0].shape, BF16),
                pltpu.SemaphoreType.DMA((len(blocks),)),
            ],
        ),
        out_shape=[
            jax.ShapeDtypeStruct(shapes[0], BF16),
            jax.ShapeDtypeStruct(shapes[1], F32 if last else BF16),
        ],
        compiler_params=pltpu.CompilerParams(vmem_limit_bytes=48 * 2**20),
    )(order, *blocks, *earlier, weight)


def finish_kernel(mine, table, *refs):
    shares, out = refs[:-1], refs[-1]
    rows = []
    for got, (_, c) in zip(shares, CHUNKS, strict=True):
        total = got[0].astype(F32)
        for j in range(1, N):
            total = total + got[j].astype(F32)
        rows.append(unpack(total, total.shape[0] * LANES // out.shape[1]).astype(BF16))
    rows = jnp.concatenate(rows, axis=0)
    size = out.shape[0]
    o = lax.broadcasted_iota(jnp.int32, (size, size), 0)
    col = lax.broadcasted_iota(jnp.int32, (size, size), 1)
    slots = REQ + 1
    step, j, slot = o // (N * slots), (o // slots) % N, o % slots
    source = size - ARRIVING + j * STEPS + step
    before = 0
    for first, c in CHUNKS:
        inside = (slot >= first) & (slot < first + c)
        source = jnp.where(inside, before + j * c * STEPS + (slot - first) * STEPS + step, source)
        before += N * c * STEPS
    c0 = CHUNKS[0][1] * STEPS
    line = table[:, 1, : N * c0]
    row = lax.broadcasted_iota(jnp.int32, line.shape, 0)
    line = jnp.sum(jnp.where(row == mine[0], line, 0.0), axis=0, keepdims=True)
    r = lax.broadcasted_iota(jnp.int32, (size, N * c0), 0)
    lane = lax.broadcasted_iota(jnp.int32, (size, N * c0), 1)
    pick_slot = ((r // slots) % N) * c0 == lane
    away = jnp.sum(jnp.where(pick_slot, line, 0.0), axis=1, keepdims=True)
    slot_of = lax.broadcasted_iota(jnp.int32, (size, 1), 0) % slots
    stays = (slot_of == REQ) | (slot_of.astype(F32) != away)
    pick = ((col == source) & stays).astype(F32).astype(BF16)
    out[...] = jnp.dot(pick, rows, preferred_element_type=F32).astype(BF16)


def finish(mine, table, shares, cols):
    vmem = pl.BlockSpec(memory_space=pltpu.VMEM)
    size = sum(s.shape[1] for s in shares) * LANES // cols
    return pl.pallas_call(
        finish_kernel,
        in_specs=[pl.BlockSpec(memory_space=pltpu.SMEM), vmem] + [vmem] * len(shares),
        out_specs=vmem,
        out_shape=jax.ShapeDtypeStruct((size, cols), BF16),
        compiler_params=pltpu.CompilerParams(vmem_limit_bytes=16 * 2**20),
    )(mine, table, *shares)


def along_z(by):
    chips = N // 2
    return [(z * 2 + c, (z + by) % chips * 2 + c) for z in range(chips) for c in range(2)]


OTHER_CORE = [(i, i ^ 1) for i in range(N)]


def gather(block):
    me = lax.axis_index("dp")
    chips = N // 2
    held = [(block, me)]
    up = down = block
    for hop in range(1, chips // 2 + 1):
        up = lax.ppermute(up, "dp", along_z(1))
        held.append((up, (me + N - 2 * hop) % N))
        if hop < chips // 2:
            down = lax.ppermute(down, "dp", along_z(-1))
            held.append((down, (me + 2 * hop) % N))
    held += [(lax.ppermute(b, "dp", OTHER_CORE), i ^ 1) for b, i in held]
    return [b for b, _ in held], jnp.stack([i for _, i in held]).astype(jnp.int32)


def across_tp(x):
    return lax.all_to_all(x, "tp", split_axis=0, concat_axis=0, tiled=True)


def shards(latent_cache, lengths, queries, new_latents, migrations, value_weight, output_weight):
    cache = jnp.swapaxes(latent_cache, 1, 2)
    asked = jnp.swapaxes(queries, 2, 3)
    weight = jnp.swapaxes(output_weight, 0, 1)
    counts = tuple(c for _, c in CHUNKS)
    sent = attend(lengths, migrations, asked, cache, new_latents)
    hidden = values(across_tp(sent), value_weight)
    blocks, order = gather(hidden[0])
    partial, table = project(counts, order, blocks, weight, [])
    shares = across_tp(partial)
    mine = lax.axis_index("tp").astype(jnp.int32).reshape(1)
    return finish(mine, table, [shares], weight.shape[0])


def solution(mesh):
    return jax.shard_map(
        shards,
        mesh=mesh,
        in_specs=(
            P(("dp", "tp"), None, None),
            P(("dp", "tp")),
            P(None, ("dp", "tp"), None, None),
            P(None, ("dp", "tp"), None),
            P(("dp", "tp"), None),
            P("tp", None, None),
            P("tp", "dp"),
        ),
        out_specs=P("tp", "dp"),
        check_vma=False,
    )
```

time: 265 us -> 115 us (0.43)
  waiting for transfers between devices: 149 us -> 42 us
  blocking collectives: 58.5 us -> 24.4 us
  starting transfers between devices: 0.13 us -> 30.4 us
  matrix products: 19.7 us -> 0 us
  between operations: 18 us -> 0.08 us
  Pallas kernels: 0 us -> 17.6 us
  local copies, waits for them, and re-layouts: 13.9 us -> 0.1 us
  other arithmetic: 5.11 us -> 0 us
    reduce_scatter x1 -> x0, waiting for transfers between devices: 77 us -> none  [shards(): lax.psum_scatter(jnp.dot(gathered, output_weight, preferred_element_type=...]
    all_gather x3 -> x0, waiting for transfers between devices: 71.5 us -> none  [the longest x1 40.3 us: shards(): gathered = lax.all_gather(flattened, 'dp', axis=0, tiled=True)]
    all_to_all x0 -> x1, waiting for transfers between devices: none -> 31.2 us  [across_tp(): return lax.all_to_all(x, 'tp', split_axis=0, concat_axis=0, tiled=True)]
    ppermute x0 -> x15, starting transfers between devices: none -> 26.6 us  [the longest x8 15.2 us: gather(): held += [(lax.ppermute(b, 'dp', OTHER_CORE), i ^ 1) for b, i in held]]
    dot_general x10 -> x0, matrix products: 19.7 us -> none  [the longest x1 6.72 us: shards(): jnp.dot(gathered, output_weight, preferred_element_type=jnp.float32)]
    all_gather x1 -> x0, blocking collectives: 18.4 us -> none  [shards(): lax.all_gather(sent_new[None], 'dp', axis=0, tiled=True)]
    pallas_call x0 -> x4, Pallas kernels: none -> 17.6 us  [the longest x1 8.41 us: attend(): pl.pallas_call(attend_kernel, grid_spec=pltpu.PrefetchScalarGridSpec(num_...]
    unnamed x1 -> x0, blocking collectives: 14.8 us -> none
  transfers between devices with their start and end apart: 4 -> 16, of which waited for: 3 -> 5; matrix products, arithmetic and copies ran while one was open for 8% -> 0% of each run, Pallas kernels for 0% -> 0%
where the time goes in v2:
time: 115 us; the launch traced here: 114 us
  waiting for transfers between devices  42 us (37%)
  starting transfers between devices  30.4 us (26%)
  blocking collectives  24.4 us (21%)
  Pallas kernels  17.6 us (15%)
    all_to_all x1, waiting for transfers between devices, across_tp(): return lax.all_to_all(x, 'tp', split_axis=0, concat_axis=0, tiled=True)  31.2 us
    all_to_all x1, blocking collectives, across_tp(): return lax.all_to_all(x, 'tp', split_axis=0, concat_axis=0, tiled=True)  24.4 us
    ppermute x8, starting transfers between devices, gather(): held += [(lax.ppermute(b, 'dp', OTHER_CORE), i ^ 1) for b, i in held]  15.2 us
    ppermute x3, starting transfers between devices, gather(): down = lax.ppermute(down, 'dp', along_z(-1))  9.68 us
    pallas_call x1, Pallas kernels, attend(): pl.pallas_call(attend_kernel, grid_spec=pltpu.PrefetchScalarGridSpec(num_...  8.41 us
    ppermute x4, waiting for transfers between devices, gather(): up = lax.ppermute(up, 'dp', along_z(1))  8.2 us
    pallas_call x1, Pallas kernels, project(): pl.pallas_call(kernel, grid_spec=pltpu.PrefetchScalarGridSpec(num_scalar_...  7.21 us
    all_to_all x1, starting transfers between devices, across_tp(): return lax.all_to_all(x, 'tp', split_axis=0, concat_axis=0, tiled=True)  3.73 us
  transfers between devices with their start and end apart: 16, of which 5 were waited for; matrix products, arithmetic and copies ran while one was open for 0% of the time, Pallas kernels for 0%

profile of v2, /device:TPU:1, one launch (start us, length us, event | category | flops | bytes accessed | tf_op | source)
XLA Modules:
  0.0 114.5 jit_solution(11185549852281105561)
XLA Ops:
  0.0 8.4 %shard_map.73 = bf16[16,272,128]{2,1,0:T(8,128)(2,1)} custom-call(s32[4]{0:T(128)} %lengths.1, s32[1,2]{1,0:T(1,128)} %moves.1, bf16[2,4,576,128]{3,2,1,0:T(8,128)(2,1)} %bitcast.22, bf16[4,576,1024]{2,1,0:T(8,128)(2,1)} %bitcast.21, bf16[2,4,576]{2,1,0:T(4,128)(2,1)} %new.1), custom_call_target="tpu_custom_call" | custom-call | tf_op jit(solution)/shard_map/pallas_call | solution.py:75
  8.4 24.4 %all_to_all.10.got = bf16[16,272,128]{2,1,0:T(8,128)(2,1)S(1)} all-to-all(bf16[16,272,128]{2,1,0:T(8,128)(2,1)} %shard_map.73), channel_id=1, replica_groups=mesh['dp'=16,'tp'=16] {'tp'}, dimensions={0} | all-to-all | bytes 2228224 | tf_op jit(solution)/shard_map/all_to_all | solution.py:339
  32.8 0.7 shard_map.74.refs_1_
  33.5 1.7 %collective-permute-start = (bf16[1040,128]{1,0:T(8,128)(2,1)S(1)}, bf16[1040,128]{1,0:T(8,128)(2,1)S(1)}, u32[]{:S(2)}, u32[]{:S(2)}) collective-permute-start(bf16[1040,128]{1,0:T(8,128)(2,1)S(1)} %shard_map.74.refs_1_), channel_id=1, source_target_pairs={{0,32},{16,48},{32,64},{48,80},{64,96},{80,112},{96,128},{112,144}... | collective-permute-start | bytes 798728 | tf_op jit(solution)/shard_map/ppermute | solution.py:329
  35.2 4.1 %collective-permute-start.1 = (bf16[1040,128]{1,0:T(8,128)(2,1)S(1)}, bf16[1040,128]{1,0:T(8,128)(2,1)S(1)}, u32[]{:S(2)}, u32[]{:S(2)}) collective-permute-start(bf16[1040,128]{1,0:T(8,128)(2,1)S(1)} %shard_map.74.refs_1_), channel_id=1, source_target_pairs={{0,224},{16,240},{32,0},{48,16},{64,32},{80,48},{96,64},{112,80},{... | collective-permute-start | bytes 798728 | tf_op jit(solution)/shard_map/ppermute | solution.py:332
  39.3 4.4 %collective-permute-done.refs_2_ = bf16[1040,128]{1,0:T(8,128)(2,1)S(1)} collective-permute-done((bf16[1040,128]{1,0:T(8,128)(2,1)S(1)}, bf16[1040,128]{1,0:T(8,128)(2,1)S(1)}, u32[]{:S(2)}, u32[]{:S(2)}) %collective-permute-start) | collective-permute-done | bytes 266272 | tf_op jit(solution)/shard_map/ppermute | solution.py:329
  43.7 2.7 %collective-permute-start.3 = (bf16[1040,128]{1,0:T(8,128)(2,1)S(1)}, bf16[1040,128]{1,0:T(8,128)(2,1)S(1)}, u32[]{:S(2)}, u32[]{:S(2)}) collective-permute-start(bf16[1040,128]{1,0:T(8,128)(2,1)S(1)} %collective-permute-done.1.refs_3_), channel_id=1, source_target_pairs={{0,224},{16,240},{32,0},{48,16},{64,32},{80,48},{96,64},{112,80},{... | collective-permute-start | bytes 798728 | tf_op jit(solution)/shard_map/ppermute | solution.py:332
  46.4 3.8 %collective-permute-done.2.refs_4_ = bf16[1040,128]{1,0:T(8,128)(2,1)S(1)} collective-permute-done((bf16[1040,128]{1,0:T(8,128)(2,1)S(1)}, bf16[1040,128]{1,0:T(8,128)(2,1)S(1)}, u32[]{:S(2)}, u32[]{:S(2)}) %collective-permute-start.2) | collective-permute-done | bytes 266272 | tf_op jit(solution)/shard_map/ppermute | solution.py:329
  50.2 4.0 %collective-permute-start.7 = (bf16[1040,128]{1,0:T(8,128)(2,1)S(1)}, bf16[1040,128]{1,0:T(8,128)(2,1)S(1)}, u32[]{:S(2)}, u32[]{:S(2)}) collective-permute-start(bf16[1040,128]{1,0:T(8,128)(2,1)S(1)} %shard_map.74.refs_1_), channel_id=1, source_target_pairs={{0,16},{16,0},{32,48},{48,32},{64,80},{80,64},{96,112},{112,96},{1... | collective-permute-start | bytes 798728 | tf_op jit(solution)/shard_map/ppermute | solution.py:334
  54.2 0.0 collective-permute-start.9
  54.2 0.5 collective-permute-start.8
  54.7 3.0 %collective-permute-start.5 = (bf16[1040,128]{1,0:T(8,128)(2,1)S(1)}, bf16[1040,128]{1,0:T(8,128)(2,1)}, u32[]{:S(2)}, u32[]{:S(2)}) collective-permute-start(bf16[1040,128]{1,0:T(8,128)(2,1)S(1)} %collective-permute-done.3.refs_5_), channel_id=1, source_target_pairs={{0,224},{16,240},{32,0},{48,16},{64,32},{80,48},{96,64},{112,80},{... | collective-permute-start | bytes 798728 | tf_op jit(solution)/shard_map/ppermute | solution.py:332
  57.7 4.2 %collective-permute-start.11 = (bf16[1040,128]{1,0:T(8,128)(2,1)S(1)}, bf16[1040,128]{1,0:T(8,128)(2,1)}, u32[]{:S(2)}, u32[]{:S(2)}) collective-permute-start(bf16[1040,128]{1,0:T(8,128)(2,1)S(1)} %collective-permute-done.3.refs_5_), channel_id=1, source_target_pairs={{0,16},{16,0},{32,48},{48,32},{64,80},{80,64},{96,112},{112,96},{1... | collective-permute-start | bytes 798728 | tf_op jit(solution)/shard_map/ppermute | solution.py:334
  61.8 0.1 collective-permute-start.10
  61.9 0.4 collective-permute-start.12
  62.3 1.1 collective-permute-done.5.refs_7_
  63.5 0.8 collective-permute-start.13
  64.3 5.3 %collective-permute-start.14 = (bf16[1040,128]{1,0:T(8,128)(2,1)}, bf16[1040,128]{1,0:T(8,128)(2,1)}, u32[]{:S(2)}, u32[]{:S(2)}) collective-permute-start(bf16[1040,128]{1,0:T(8,128)(2,1)} %collective-permute-done.6.refs_8_), channel_id=1, source_target_pairs={{0,16},{16,0},{32,48},{48,32},{64,80},{80,64},{96,112},{112,96},{1... | collective-permute-start | bytes 798728 | tf_op jit(solution)/shard_map/ppermute | solution.py:334
  69.5 0.1 stack.67.refs_0_
  69.7 1.4 %collective-permute-done.14.refs_16_ = bf16[1040,128]{1,0:T(8,128)(2,1)} collective-permute-done((bf16[1040,128]{1,0:T(8,128)(2,1)}, bf16[1040,128]{1,0:T(8,128)(2,1)}, u32[]{:S(2)}, u32[]{:S(2)}) %collective-permute-start.14) | collective-permute-done | bytes 266272 | tf_op jit(solution)/shard_map/ppermute | solution.py:334
  71.0 7.2 %shard_map.75 = (bf16[16,560,128]{2,1,0:T(8,128)(2,1)}, f32[16,16,128]{2,1,0:T(8,128)S(1)}) custom-call(s32[16]{0:T(128)S(1)} %stack.67.refs_0_, bf16[1040,128]{1,0:T(8,128)(2,1)S(1)} %shard_map.74.refs_1_, bf16[1040,128]{1,0:T(8,128)(2,1)S(1)} %collective-permute-done.refs_2_, bf16[1040,128]{1,0:T(8,128)(2,1)S(1)} %collective-permute-done.1.refs_3_, ...), custom_call_target="tpu_custom_call" | custom-call | tf_op jit(solution)/shard_map/pallas_call | solution.py:247
  78.3 3.7 %all-to-all-start.1 = ((bf16[16,560,128]{2,1,0:T(8,128)(2,1)}), bf16[16,560,128]{2,1,0:T(8,128)(2,1)S(1)}, u32[]{:S(2)}, u32[]{:S(2)}) async-start(bf16[16,560,128]{2,1,0:T(8,128)(2,1)} %get-tuple-element.8), calls=%async_computation.1 | async-start | bytes 4587520 | tf_op jit(solution)/shard_map/all_to_all | solution.py:339
  82.0 31.2 %all-to-all-done.1.refs_0_ = bf16[16,560,128]{2,1,0:T(8,128)(2,1)S(1)} async-done(((bf16[16,560,128]{2,1,0:T(8,128)(2,1)}), bf16[16,560,128]{2,1,0:T(8,128)(2,1)S(1)}, u32[]{:S(2)}, u32[]{:S(2)}) %all-to-all-start.1) | async-done | bytes 2293792 | tf_op jit(solution)/shard_map/all_to_all | solution.py:339
  113.3 1.2 %shard_map.76 = bf16[160,448]{1,0:T(8,128)(2,1)} custom-call(s32[1]{0:T(128)} %bitcast.mine, f32[16,16,128]{2,1,0:T(8,128)S(1)} %get-tuple-element.7.table, bf16[16,560,128]{2,1,0:T(8,128)(2,1)S(1)} %all-to-all-done.1.refs_0_), custom_call_target="tpu_custom_call" | custom-call | tf_op jit(solution)/shard_map/pallas_call | solution.py:306
  (18 shorter events, 0.0 us)
Async XLA Ops:
  8.4 24.4 %copy-start = (bf16[8,512,128]{2,1,0:T(8,128)(2,1)S(1)}, bf16[8,512,128]{2,1,0:T(8,128)(2,1)}, u32[]{:S(2)}) copy-start(bf16[8,512,128]{2,1,0:T(8,128)(2,1)} %weight.1) | copy-start | bytes 3145732
  8.4 62.6 %copy-start.1 = (bf16[1024,448]{0,1:T(8,128)(2,1)S(1)}, bf16[1024,448]{0,1:T(8,128)(2,1)}, u32[]{:S(2)}) copy-start(bf16[1024,448]{0,1:T(8,128)(2,1)} %param.13) | copy-start | bytes 2752516
  33.5 10.2 %collective-permute-start = (bf16[1040,128]{1,0:T(8,128)(2,1)S(1)}, bf16[1040,128]{1,0:T(8,128)(2,1)S(1)}, u32[]{:S(2)}, u32[]{:S(2)}) collective-permute-start(bf16[1040,128]{1,0:T(8,128)(2,1)S(1)} %shard_map.74.refs_1_), channel_id=1, source_target_pairs={{0,32},{16,48},{32,64},{48,80},{64,96},{80,112},{96,128},{112,144}... | collective-permute-start | bytes 798728 | tf_op jit(solution)/shard_map/ppermute | solution.py:329
  35.2 8.5 %collective-permute-start.1 = (bf16[1040,128]{1,0:T(8,128)(2,1)S(1)}, bf16[1040,128]{1,0:T(8,128)(2,1)S(1)}, u32[]{:S(2)}, u32[]{:S(2)}) collective-permute-start(bf16[1040,128]{1,0:T(8,128)(2,1)S(1)} %shard_map.74.refs_1_), channel_id=1, source_target_pairs={{0,224},{16,240},{32,0},{48,16},{64,32},{80,48},{96,64},{112,80},{... | collective-permute-start | bytes 798728 | tf_op jit(solution)/shard_map/ppermute | solution.py:332
  43.7 6.5 %collective-permute-start.2 = (bf16[1040,128]{1,0:T(8,128)(2,1)S(1)}, bf16[1040,128]{1,0:T(8,128)(2,1)S(1)}, u32[]{:S(2)}, u32[]{:S(2)}) collective-permute-start(bf16[1040,128]{1,0:T(8,128)(2,1)S(1)} %collective-permute-done.refs_2_), channel_id=1, source_target_pairs={{0,32},{16,48},{32,64},{48,80},{64,96},{80,112},{96,128},{112,144}... | collective-permute-start | bytes 798728 | tf_op jit(solution)/shard_map/ppermute | solution.py:329
  43.7 11.0 %collective-permute-start.3 = (bf16[1040,128]{1,0:T(8,128)(2,1)S(1)}, bf16[1040,128]{1,0:T(8,128)(2,1)S(1)}, u32[]{:S(2)}, u32[]{:S(2)}) collective-permute-start(bf16[1040,128]{1,0:T(8,128)(2,1)S(1)} %collective-permute-done.1.refs_3_), channel_id=1, source_target_pairs={{0,224},{16,240},{32,0},{48,16},{64,32},{80,48},{96,64},{112,80},{... | collective-permute-start | bytes 798728 | tf_op jit(solution)/shard_map/ppermute | solution.py:332
  50.2 7.5 %collective-permute-start.4 = (bf16[1040,128]{1,0:T(8,128)(2,1)S(1)}, bf16[1040,128]{1,0:T(8,128)(2,1)S(1)}, u32[]{:S(2)}, u32[]{:S(2)}) collective-permute-start(bf16[1040,128]{1,0:T(8,128)(2,1)S(1)} %collective-permute-done.2.refs_4_), channel_id=1, source_target_pairs={{0,32},{16,48},{32,64},{48,80},{64,96},{80,112},{96,128},{112,144}... | collective-permute-start | bytes 798728 | tf_op jit(solution)/shard_map/ppermute | solution.py:329
  50.2 7.5 %collective-permute-start.7 = (bf16[1040,128]{1,0:T(8,128)(2,1)S(1)}, bf16[1040,128]{1,0:T(8,128)(2,1)S(1)}, u32[]{:S(2)}, u32[]{:S(2)}) collective-permute-start(bf16[1040,128]{1,0:T(8,128)(2,1)S(1)} %shard_map.74.refs_1_), channel_id=1, source_target_pairs={{0,16},{16,0},{32,48},{48,32},{64,80},{80,64},{96,112},{112,96},{1... | collective-permute-start | bytes 798728 | tf_op jit(solution)/shard_map/ppermute | solution.py:334
  54.2 7.6 %collective-permute-start.9 = (bf16[1040,128]{1,0:T(8,128)(2,1)S(1)}, bf16[1040,128]{1,0:T(8,128)(2,1)S(1)}, u32[]{:S(2)}, u32[]{:S(2)}) collective-permute-start(bf16[1040,128]{1,0:T(8,128)(2,1)S(1)} %collective-permute-done.1.refs_3_), channel_id=1, source_target_pairs={{0,16},{16,0},{32,48},{48,32},{64,80},{80,64},{96,112},{112,96},{1... | collective-permute-start | bytes 798728 | tf_op jit(solution)/shard_map/ppermute | solution.py:334
  54.2 7.7 %collective-permute-start.8 = (bf16[1040,128]{1,0:T(8,128)(2,1)S(1)}, bf16[1040,128]{1,0:T(8,128)(2,1)S(1)}, u32[]{:S(2)}, u32[]{:S(2)}) collective-permute-start(bf16[1040,128]{1,0:T(8,128)(2,1)S(1)} %collective-permute-done.refs_2_), channel_id=1, source_target_pairs={{0,16},{16,0},{32,48},{48,32},{64,80},{80,64},{96,112},{112,96},{1... | collective-permute-start | bytes 798728 | tf_op jit(solution)/shard_map/ppermute | solution.py:334
  54.7 8.8 %collective-permute-start.5 = (bf16[1040,128]{1,0:T(8,128)(2,1)S(1)}, bf16[1040,128]{1,0:T(8,128)(2,1)}, u32[]{:S(2)}, u32[]{:S(2)}) collective-permute-start(bf16[1040,128]{1,0:T(8,128)(2,1)S(1)} %collective-permute-done.3.refs_5_), channel_id=1, source_target_pairs={{0,224},{16,240},{32,0},{48,16},{64,32},{80,48},{96,64},{112,80},{... | collective-permute-start | bytes 798728 | tf_op jit(solution)/shard_map/ppermute | solution.py:332
  57.7 6.6 %collective-permute-start.6 = (bf16[1040,128]{1,0:T(8,128)(2,1)S(1)}, bf16[1040,128]{1,0:T(8,128)(2,1)}, u32[]{:S(2)}, u32[]{:S(2)}) collective-permute-start(bf16[1040,128]{1,0:T(8,128)(2,1)S(1)} %collective-permute-done.4.refs_6_), channel_id=1, source_target_pairs={{0,32},{16,48},{32,64},{48,80},{64,96},{80,112},{96,128},{112,144}... | collective-permute-start | bytes 798728 | tf_op jit(solution)/shard_map/ppermute | solution.py:329
  57.7 12.0 %collective-permute-start.11 = (bf16[1040,128]{1,0:T(8,128)(2,1)S(1)}, bf16[1040,128]{1,0:T(8,128)(2,1)}, u32[]{:S(2)}, u32[]{:S(2)}) collective-permute-start(bf16[1040,128]{1,0:T(8,128)(2,1)S(1)} %collective-permute-done.3.refs_5_), channel_id=1, source_target_pairs={{0,16},{16,0},{32,48},{48,32},{64,80},{80,64},{96,112},{112,96},{1... | collective-permute-start | bytes 798728 | tf_op jit(solution)/shard_map/ppermute | solution.py:334
  61.8 7.8 %collective-permute-start.10 = (bf16[1040,128]{1,0:T(8,128)(2,1)S(1)}, bf16[1040,128]{1,0:T(8,128)(2,1)}, u32[]{:S(2)}, u32[]{:S(2)}) collective-permute-start(bf16[1040,128]{1,0:T(8,128)(2,1)S(1)} %collective-permute-done.2.refs_4_), channel_id=1, source_target_pairs={{0,16},{16,0},{32,48},{48,32},{64,80},{80,64},{96,112},{112,96},{1... | collective-permute-start | bytes 798728 | tf_op jit(solution)/shard_map/ppermute | solution.py:334
  61.9 7.7 %collective-permute-start.12 = (bf16[1040,128]{1,0:T(8,128)(2,1)S(1)}, bf16[1040,128]{1,0:T(8,128)(2,1)}, u32[]{:S(2)}, u32[]{:S(2)}) collective-permute-start(bf16[1040,128]{1,0:T(8,128)(2,1)S(1)} %collective-permute-done.4.refs_6_), channel_id=1, source_target_pairs={{0,16},{16,0},{32,48},{48,32},{64,80},{80,64},{96,112},{112,96},{1... | collective-permute-start | bytes 798728 | tf_op jit(solution)/shard_map/ppermute | solution.py:334
  63.5 6.2 %collective-permute-start.13 = (bf16[1040,128]{1,0:T(8,128)(2,1)}, bf16[1040,128]{1,0:T(8,128)(2,1)}, u32[]{:S(2)}, u32[]{:S(2)}) collective-permute-start(bf16[1040,128]{1,0:T(8,128)(2,1)} %collective-permute-done.5.refs_7_), channel_id=1, source_target_pairs={{0,16},{16,0},{32,48},{48,32},{64,80},{80,64},{96,112},{112,96},{1... | collective-permute-start | bytes 798728 | tf_op jit(solution)/shard_map/ppermute | solution.py:334
  64.3 6.8 %collective-permute-start.14 = (bf16[1040,128]{1,0:T(8,128)(2,1)}, bf16[1040,128]{1,0:T(8,128)(2,1)}, u32[]{:S(2)}, u32[]{:S(2)}) collective-permute-start(bf16[1040,128]{1,0:T(8,128)(2,1)} %collective-permute-done.6.refs_8_), channel_id=1, source_target_pairs={{0,16},{16,0},{32,48},{48,32},{64,80},{80,64},{96,112},{112,96},{1... | collective-permute-start | bytes 798728 | tf_op jit(solution)/shard_map/ppermute | solution.py:334
  78.3 35.0 %all-to-all-start.1 = ((bf16[16,560,128]{2,1,0:T(8,128)(2,1)}), bf16[16,560,128]{2,1,0:T(8,128)(2,1)S(1)}, u32[]{:S(2)}, u32[]{:S(2)}) async-start(bf16[16,560,128]{2,1,0:T(8,128)(2,1)} %get-tuple-element.8), calls=%async_computation.1 | async-start | bytes 4587520 | tf_op jit(solution)/shard_map/all_to_all | solution.py:339

commit v3 on v2

--- a/solution.py
+++ b/solution.py
@@ -40,7 +40,7 @@
     total = jnp.sum(far, axis=1, keepdims=True) + jnp.sum(near, axis=1, keepdims=True)
     mixed = lax.dot_general(far.astype(BF16), keys[:VAL], NT, preferred_element_type=F32)
     mixed = mixed + jnp.dot(near.astype(BF16), own[:, :VAL], preferred_element_type=F32)
-    return mixed / total
+    return mixed * (1.0 / total)
 
 
 def attend_kernel(lengths, moves, query, cache, new, out):
@@ -348,8 +348,9 @@
     hidden = values(across_tp(sent), value_weight)
     blocks, order = gather(hidden[0])
     partial, table = project(counts, order, blocks, weight, [])
+    mine = lax.axis_index("tp").astype(jnp.int32).reshape(1)
+    partial, table, mine = lax.optimization_barrier((partial, table, mine))
     shares = across_tp(partial)
-    mine = lax.axis_index("tp").astype(jnp.int32).reshape(1)
     return finish(mine, table, [shares], weight.shape[0])
 
 

time: 115 us -> 113 us (0.983)
  blocking collectives: 24.4 us -> 57.6 us
  waiting for transfers between devices: 42 us -> 10.7 us
  starting transfers between devices: 30.4 us -> 26.6 us
    all_to_all x1 -> x2, blocking collectives: 24.4 us -> 57.6 us  [across_tp(): return lax.all_to_all(x, 'tp', split_axis=0, concat_axis=0, tiled=True)]
    all_to_all x1 -> x0, waiting for transfers between devices: 31.2 us -> none  [across_tp(): return lax.all_to_all(x, 'tp', split_axis=0, concat_axis=0, tiled=True)]
    all_to_all x1 -> x0, starting transfers between devices: 3.73 us -> none  [across_tp(): return lax.all_to_all(x, 'tp', split_axis=0, concat_axis=0, tiled=True)]
  transfers between devices with their start and end apart: 16 -> 15, of which waited for: 5 -> 4; matrix products, arithmetic and copies ran while one was open for 0% -> 0% of each run, Pallas kernels for 0% -> 0%
where the time goes in v3:
time: 113 us
  blocking collectives  57.6 us (51%)
  starting transfers between devices  26.6 us (24%)
  Pallas kernels  17.6 us (16%)
  waiting for transfers between devices  10.7 us (9%)
    all_to_all x2, blocking collectives, across_tp(): return lax.all_to_all(x, 'tp', split_axis=0, concat_axis=0, tiled=True)  57.6 us
    ppermute x8, starting transfers between devices, gather(): held += [(lax.ppermute(b, 'dp', OTHER_CORE), i ^ 1) for b, i in held]  15.2 us
    ppermute x3, starting transfers between devices, gather(): down = lax.ppermute(down, 'dp', along_z(-1))  9.68 us
    pallas_call x1, Pallas kernels, attend(): pl.pallas_call(attend_kernel, grid_spec=pltpu.PrefetchScalarGridSpec(num_...  8.4 us
    ppermute x4, waiting for transfers between devices, gather(): up = lax.ppermute(up, 'dp', along_z(1))  8.2 us
    pallas_call x1, Pallas kernels, project(): pl.pallas_call(kernel, grid_spec=pltpu.PrefetchScalarGridSpec(num_scalar_...  7.2 us
  transfers between devices with their start and end apart: 15, of which 4 were waited for; matrix products, arithmetic and copies ran while one was open for 0% of the time, Pallas kernels for 0%

profile of v3, /device:TPU:1, one launch (start us, length us, event | category | flops | bytes accessed | tf_op | source)
XLA Modules:
  0.0 112.7 jit_solution(9086268850323171855)
XLA Ops:
  0.0 8.4 %shard_map.73 = bf16[16,272,128]{2,1,0:T(8,128)(2,1)} custom-call(s32[4]{0:T(128)} %lengths.1, s32[1,2]{1,0:T(1,128)} %moves.1, bf16[2,4,576,128]{3,2,1,0:T(8,128)(2,1)} %bitcast.22, bf16[4,576,1024]{2,1,0:T(8,128)(2,1)} %bitcast.21, bf16[2,4,576]{2,1,0:T(4,128)(2,1)} %new.1), custom_call_target="tpu_custom_call" | custom-call | tf_op jit(solution)/shard_map/pallas_call | solution.py:75
  8.4 24.4 %all_to_all.10.got = bf16[16,272,128]{2,1,0:T(8,128)(2,1)S(1)} all-to-all(bf16[16,272,128]{2,1,0:T(8,128)(2,1)} %shard_map.73), channel_id=1, replica_groups=mesh['dp'=16,'tp'=16] {'tp'}, dimensions={0} | all-to-all | bytes 2228224 | tf_op jit(solution)/shard_map/all_to_all | solution.py:339
  32.8 0.7 shard_map.74.refs_1_
  33.5 1.7 %collective-permute-start = (bf16[1040,128]{1,0:T(8,128)(2,1)S(1)}, bf16[1040,128]{1,0:T(8,128)(2,1)S(1)}, u32[]{:S(2)}, u32[]{:S(2)}) collective-permute-start(bf16[1040,128]{1,0:T(8,128)(2,1)S(1)} %shard_map.74.refs_1_), channel_id=1, source_target_pairs={{0,32},{16,48},{32,64},{48,80},{64,96},{80,112},{96,128},{112,144}... | collective-permute-start | bytes 798728 | tf_op jit(solution)/shard_map/ppermute | solution.py:329
  35.2 4.1 %collective-permute-start.1 = (bf16[1040,128]{1,0:T(8,128)(2,1)S(1)}, bf16[1040,128]{1,0:T(8,128)(2,1)S(1)}, u32[]{:S(2)}, u32[]{:S(2)}) collective-permute-start(bf16[1040,128]{1,0:T(8,128)(2,1)S(1)} %shard_map.74.refs_1_), channel_id=1, source_target_pairs={{0,224},{16,240},{32,0},{48,16},{64,32},{80,48},{96,64},{112,80},{... | collective-permute-start | bytes 798728 | tf_op jit(solution)/shard_map/ppermute | solution.py:332
  39.3 4.4 %collective-permute-done.refs_2_ = bf16[1040,128]{1,0:T(8,128)(2,1)S(1)} collective-permute-done((bf16[1040,128]{1,0:T(8,128)(2,1)S(1)}, bf16[1040,128]{1,0:T(8,128)(2,1)S(1)}, u32[]{:S(2)}, u32[]{:S(2)}) %collective-permute-start) | collective-permute-done | bytes 266272 | tf_op jit(solution)/shard_map/ppermute | solution.py:329
  43.7 2.7 %collective-permute-start.3 = (bf16[1040,128]{1,0:T(8,128)(2,1)S(1)}, bf16[1040,128]{1,0:T(8,128)(2,1)S(1)}, u32[]{:S(2)}, u32[]{:S(2)}) collective-permute-start(bf16[1040,128]{1,0:T(8,128)(2,1)S(1)} %collective-permute-done.1.refs_3_), channel_id=1, source_target_pairs={{0,224},{16,240},{32,0},{48,16},{64,32},{80,48},{96,64},{112,80},{... | collective-permute-start | bytes 798728 | tf_op jit(solution)/shard_map/ppermute | solution.py:332
  46.4 3.8 %collective-permute-done.2.refs_4_ = bf16[1040,128]{1,0:T(8,128)(2,1)S(1)} collective-permute-done((bf16[1040,128]{1,0:T(8,128)(2,1)S(1)}, bf16[1040,128]{1,0:T(8,128)(2,1)S(1)}, u32[]{:S(2)}, u32[]{:S(2)}) %collective-permute-start.2) | collective-permute-done | bytes 266272 | tf_op jit(solution)/shard_map/ppermute | solution.py:329
  50.2 0.0 collective-permute-start.4
  50.2 4.0 %collective-permute-start.7 = (bf16[1040,128]{1,0:T(8,128)(2,1)S(1)}, bf16[1040,128]{1,0:T(8,128)(2,1)S(1)}, u32[]{:S(2)}, u32[]{:S(2)}) collective-permute-start(bf16[1040,128]{1,0:T(8,128)(2,1)S(1)} %shard_map.74.refs_1_), channel_id=1, source_target_pairs={{0,16},{16,0},{32,48},{48,32},{64,80},{80,64},{96,112},{112,96},{1... | collective-permute-start | bytes 798728 | tf_op jit(solution)/shard_map/ppermute | solution.py:334
  54.2 0.0 collective-permute-start.9
  54.2 0.5 collective-permute-start.8
  54.7 3.0 %collective-permute-start.5 = (bf16[1040,128]{1,0:T(8,128)(2,1)S(1)}, bf16[1040,128]{1,0:T(8,128)(2,1)}, u32[]{:S(2)}, u32[]{:S(2)}) collective-permute-start(bf16[1040,128]{1,0:T(8,128)(2,1)S(1)} %collective-permute-done.3.refs_5_), channel_id=1, source_target_pairs={{0,224},{16,240},{32,0},{48,16},{64,32},{80,48},{96,64},{112,80},{... | collective-permute-start | bytes 798728 | tf_op jit(solution)/shard_map/ppermute | solution.py:332
  57.7 4.2 %collective-permute-start.11 = (bf16[1040,128]{1,0:T(8,128)(2,1)S(1)}, bf16[1040,128]{1,0:T(8,128)(2,1)}, u32[]{:S(2)}, u32[]{:S(2)}) collective-permute-start(bf16[1040,128]{1,0:T(8,128)(2,1)S(1)} %collective-permute-done.3.refs_5_), channel_id=1, source_target_pairs={{0,16},{16,0},{32,48},{48,32},{64,80},{80,64},{96,112},{112,96},{1... | collective-permute-start | bytes 798728 | tf_op jit(solution)/shard_map/ppermute | solution.py:334
  61.8 0.1 collective-permute-start.10
  61.9 0.4 collective-permute-start.12
  62.3 1.1 %collective-permute-done.5.refs_7_ = bf16[1040,128]{1,0:T(8,128)(2,1)} collective-permute-done((bf16[1040,128]{1,0:T(8,128)(2,1)S(1)}, bf16[1040,128]{1,0:T(8,128)(2,1)}, u32[]{:S(2)}, u32[]{:S(2)}) %collective-permute-start.5) | collective-permute-done | bytes 266272 | tf_op jit(solution)/shard_map/ppermute | solution.py:332
  63.5 0.8 collective-permute-start.13
  64.3 5.3 %collective-permute-start.14 = (bf16[1040,128]{1,0:T(8,128)(2,1)}, bf16[1040,128]{1,0:T(8,128)(2,1)}, u32[]{:S(2)}, u32[]{:S(2)}) collective-permute-start(bf16[1040,128]{1,0:T(8,128)(2,1)} %collective-permute-done.6.refs_8_), channel_id=1, source_target_pairs={{0,16},{16,0},{32,48},{48,32},{64,80},{80,64},{96,112},{112,96},{1... | collective-permute-start | bytes 798728 | tf_op jit(solution)/shard_map/ppermute | solution.py:334
  69.5 0.1 stack.67.refs_0_
  69.7 1.4 %collective-permute-done.14.refs_16_ = bf16[1040,128]{1,0:T(8,128)(2,1)} collective-permute-done((bf16[1040,128]{1,0:T(8,128)(2,1)}, bf16[1040,128]{1,0:T(8,128)(2,1)}, u32[]{:S(2)}, u32[]{:S(2)}) %collective-permute-start.14) | collective-permute-done | bytes 266272 | tf_op jit(solution)/shard_map/ppermute | solution.py:334
  71.0 7.2 %shard_map.75 = (bf16[16,560,128]{2,1,0:T(8,128)(2,1)}, f32[16,16,128]{2,1,0:T(8,128)S(1)}) custom-call(s32[16]{0:T(128)S(1)} %stack.67.refs_0_, bf16[1040,128]{1,0:T(8,128)(2,1)S(1)} %shard_map.74.refs_1_, bf16[1040,128]{1,0:T(8,128)(2,1)S(1)} %collective-permute-done.refs_2_, bf16[1040,128]{1,0:T(8,128)(2,1)S(1)} %collective-permute-done.1.refs_3_, ...), custom_call_target="tpu_custom_call" | custom-call | tf_op jit(solution)/shard_map/pallas_call | solution.py:247
  78.3 33.2 %all_to_all.11.refs_0_ = bf16[16,560,128]{2,1,0:T(8,128)(2,1)S(1)} all-to-all(bf16[16,560,128]{2,1,0:T(8,128)(2,1)} %get-tuple-element.14), channel_id=1, replica_groups=mesh['dp'=16,'tp'=16] {'tp'}, dimensions={0} | all-to-all | bytes 4587520 | tf_op jit(solution)/shard_map/all_to_all | solution.py:339
  111.5 1.2 %shard_map.76 = bf16[160,448]{1,0:T(8,128)(2,1)} custom-call(s32[1]{0:T(128)} %bitcast.19.mine, f32[16,16,128]{2,1,0:T(8,128)S(1)} %get-tuple-element.13.table, bf16[16,560,128]{2,1,0:T(8,128)(2,1)S(1)} %all_to_all.11.refs_0_), custom_call_target="tpu_custom_call" | custom-call | tf_op jit(solution)/shard_map/pallas_call | solution.py:306
  (17 shorter events, 0.0 us)
Async XLA Ops:
  8.4 24.4 %copy-start = (bf16[8,512,128]{2,1,0:T(8,128)(2,1)S(1)}, bf16[8,512,128]{2,1,0:T(8,128)(2,1)}, u32[]{:S(2)}) copy-start(bf16[8,512,128]{2,1,0:T(8,128)(2,1)} %weight.1) | copy-start | bytes 3145732
  8.4 62.6 %copy-start.1 = (bf16[1024,448]{0,1:T(8,128)(2,1)S(1)}, bf16[1024,448]{0,1:T(8,128)(2,1)}, u32[]{:S(2)}) copy-start(bf16[1024,448]{0,1:T(8,128)(2,1)} %param.13) | copy-start | bytes 2752516
  33.5 10.2 %collective-permute-start = (bf16[1040,128]{1,0:T(8,128)(2,1)S(1)}, bf16[1040,128]{1,0:T(8,128)(2,1)S(1)}, u32[]{:S(2)}, u32[]{:S(2)}) collective-permute-start(bf16[1040,128]{1,0:T(8,128)(2,1)S(1)} %shard_map.74.refs_1_), channel_id=1, source_target_pairs={{0,32},{16,48},{32,64},{48,80},{64,96},{80,112},{96,128},{112,144}... | collective-permute-start | bytes 798728 | tf_op jit(solution)/shard_map/ppermute | solution.py:329
  35.2 8.5 %collective-permute-start.1 = (bf16[1040,128]{1,0:T(8,128)(2,1)S(1)}, bf16[1040,128]{1,0:T(8,128)(2,1)S(1)}, u32[]{:S(2)}, u32[]{:S(2)}) collective-permute-start(bf16[1040,128]{1,0:T(8,128)(2,1)S(1)} %shard_map.74.refs_1_), channel_id=1, source_target_pairs={{0,224},{16,240},{32,0},{48,16},{64,32},{80,48},{96,64},{112,80},{... | collective-permute-start | bytes 798728 | tf_op jit(solution)/shard_map/ppermute | solution.py:332
  43.7 6.5 %collective-permute-start.2 = (bf16[1040,128]{1,0:T(8,128)(2,1)S(1)}, bf16[1040,128]{1,0:T(8,128)(2,1)S(1)}, u32[]{:S(2)}, u32[]{:S(2)}) collective-permute-start(bf16[1040,128]{1,0:T(8,128)(2,1)S(1)} %collective-permute-done.refs_2_), channel_id=1, source_target_pairs={{0,32},{16,48},{32,64},{48,80},{64,96},{80,112},{96,128},{112,144}... | collective-permute-start | bytes 798728 | tf_op jit(solution)/shard_map/ppermute | solution.py:329
  43.7 11.0 %collective-permute-start.3 = (bf16[1040,128]{1,0:T(8,128)(2,1)S(1)}, bf16[1040,128]{1,0:T(8,128)(2,1)S(1)}, u32[]{:S(2)}, u32[]{:S(2)}) collective-permute-start(bf16[1040,128]{1,0:T(8,128)(2,1)S(1)} %collective-permute-done.1.refs_3_), channel_id=1, source_target_pairs={{0,224},{16,240},{32,0},{48,16},{64,32},{80,48},{96,64},{112,80},{... | collective-permute-start | bytes 798728 | tf_op jit(solution)/shard_map/ppermute | solution.py:332
  50.2 7.5 %collective-permute-start.4 = (bf16[1040,128]{1,0:T(8,128)(2,1)S(1)}, bf16[1040,128]{1,0:T(8,128)(2,1)S(1)}, u32[]{:S(2)}, u32[]{:S(2)}) collective-permute-start(bf16[1040,128]{1,0:T(8,128)(2,1)S(1)} %collective-permute-done.2.refs_4_), channel_id=1, source_target_pairs={{0,32},{16,48},{32,64},{48,80},{64,96},{80,112},{96,128},{112,144}... | collective-permute-start | bytes 798728 | tf_op jit(solution)/shard_map/ppermute | solution.py:329
  50.2 7.5 %collective-permute-start.7 = (bf16[1040,128]{1,0:T(8,128)(2,1)S(1)}, bf16[1040,128]{1,0:T(8,128)(2,1)S(1)}, u32[]{:S(2)}, u32[]{:S(2)}) collective-permute-start(bf16[1040,128]{1,0:T(8,128)(2,1)S(1)} %shard_map.74.refs_1_), channel_id=1, source_target_pairs={{0,16},{16,0},{32,48},{48,32},{64,80},{80,64},{96,112},{112,96},{1... | collective-permute-start | bytes 798728 | tf_op jit(solution)/shard_map/ppermute | solution.py:334
  54.2 7.6 %collective-permute-start.9 = (bf16[1040,128]{1,0:T(8,128)(2,1)S(1)}, bf16[1040,128]{1,0:T(8,128)(2,1)S(1)}, u32[]{:S(2)}, u32[]{:S(2)}) collective-permute-start(bf16[1040,128]{1,0:T(8,128)(2,1)S(1)} %collective-permute-done.1.refs_3_), channel_id=1, source_target_pairs={{0,16},{16,0},{32,48},{48,32},{64,80},{80,64},{96,112},{112,96},{1... | collective-permute-start | bytes 798728 | tf_op jit(solution)/shard_map/ppermute | solution.py:334
  54.2 7.7 %collective-permute-start.8 = (bf16[1040,128]{1,0:T(8,128)(2,1)S(1)}, bf16[1040,128]{1,0:T(8,128)(2,1)S(1)}, u32[]{:S(2)}, u32[]{:S(2)}) collective-permute-start(bf16[1040,128]{1,0:T(8,128)(2,1)S(1)} %collective-permute-done.refs_2_), channel_id=1, source_target_pairs={{0,16},{16,0},{32,48},{48,32},{64,80},{80,64},{96,112},{112,96},{1... | collective-permute-start | bytes 798728 | tf_op jit(solution)/shard_map/ppermute | solution.py:334
  54.7 8.8 %collective-permute-start.5 = (bf16[1040,128]{1,0:T(8,128)(2,1)S(1)}, bf16[1040,128]{1,0:T(8,128)(2,1)}, u32[]{:S(2)}, u32[]{:S(2)}) collective-permute-start(bf16[1040,128]{1,0:T(8,128)(2,1)S(1)} %collective-permute-done.3.refs_5_), channel_id=1, source_target_pairs={{0,224},{16,240},{32,0},{48,16},{64,32},{80,48},{96,64},{112,80},{... | collective-permute-start | bytes 798728 | tf_op jit(solution)/shard_map/ppermute | solution.py:332
  57.6 6.6 %collective-permute-start.6 = (bf16[1040,128]{1,0:T(8,128)(2,1)S(1)}, bf16[1040,128]{1,0:T(8,128)(2,1)}, u32[]{:S(2)}, u32[]{:S(2)}) collective-permute-start(bf16[1040,128]{1,0:T(8,128)(2,1)S(1)} %collective-permute-done.4.refs_6_), channel_id=1, source_target_pairs={{0,32},{16,48},{32,64},{48,80},{64,96},{80,112},{96,128},{112,144}... | collective-permute-start | bytes 798728 | tf_op jit(solution)/shard_map/ppermute | solution.py:329
  57.7 12.0 %collective-permute-start.11 = (bf16[1040,128]{1,0:T(8,128)(2,1)S(1)}, bf16[1040,128]{1,0:T(8,128)(2,1)}, u32[]{:S(2)}, u32[]{:S(2)}) collective-permute-start(bf16[1040,128]{1,0:T(8,128)(2,1)S(1)} %collective-permute-done.3.refs_5_), channel_id=1, source_target_pairs={{0,16},{16,0},{32,48},{48,32},{64,80},{80,64},{96,112},{112,96},{1... | collective-permute-start | bytes 798728 | tf_op jit(solution)/shard_map/ppermute | solution.py:334
  61.8 7.8 %collective-permute-start.10 = (bf16[1040,128]{1,0:T(8,128)(2,1)S(1)}, bf16[1040,128]{1,0:T(8,128)(2,1)}, u32[]{:S(2)}, u32[]{:S(2)}) collective-permute-start(bf16[1040,128]{1,0:T(8,128)(2,1)S(1)} %collective-permute-done.2.refs_4_), channel_id=1, source_target_pairs={{0,16},{16,0},{32,48},{48,32},{64,80},{80,64},{96,112},{112,96},{1... | collective-permute-start | bytes 798728 | tf_op jit(solution)/shard_map/ppermute | solution.py:334
  61.9 7.7 %collective-permute-start.12 = (bf16[1040,128]{1,0:T(8,128)(2,1)S(1)}, bf16[1040,128]{1,0:T(8,128)(2,1)}, u32[]{:S(2)}, u32[]{:S(2)}) collective-permute-start(bf16[1040,128]{1,0:T(8,128)(2,1)S(1)} %collective-permute-done.4.refs_6_), channel_id=1, source_target_pairs={{0,16},{16,0},{32,48},{48,32},{64,80},{80,64},{96,112},{112,96},{1... | collective-permute-start | bytes 798728 | tf_op jit(solution)/shard_map/ppermute | solution.py:334
  63.5 6.2 %collective-permute-start.13 = (bf16[1040,128]{1,0:T(8,128)(2,1)}, bf16[1040,128]{1,0:T(8,128)(2,1)}, u32[]{:S(2)}, u32[]{:S(2)}) collective-permute-start(bf16[1040,128]{1,0:T(8,128)(2,1)} %collective-permute-done.5.refs_7_), channel_id=1, source_target_pairs={{0,16},{16,0},{32,48},{48,32},{64,80},{80,64},{96,112},{112,96},{1... | collective-permute-start | bytes 798728 | tf_op jit(solution)/shard_map/ppermute | solution.py:334
  64.3 6.8 %collective-permute-start.14 = (bf16[1040,128]{1,0:T(8,128)(2,1)}, bf16[1040,128]{1,0:T(8,128)(2,1)}, u32[]{:S(2)}, u32[]{:S(2)}) collective-permute-start(bf16[1040,128]{1,0:T(8,128)(2,1)} %collective-permute-done.6.refs_8_), channel_id=1, source_target_pairs={{0,16},{16,0},{32,48},{48,32},{64,80},{80,64},{96,112},{112,96},{1... | collective-permute-start | bytes 798728 | tf_op jit(solution)/shard_map/ppermute | solution.py:334

commit v4 on v3

--- a/solution.py
+++ b/solution.py
@@ -18,6 +18,9 @@
 META = 16
 LANES = 128
 CHUNKS = ((0, 4),)
+CELL = REQ * STEPS
+HOME = N * CELL
+AT_ONCE = 8
 ARRIVING = N * STEPS
 TOGETHER = 2
 F32 = jnp.float32
@@ -164,135 +167,114 @@
         at += part.shape[1]
 
 
-def fetch(order, blocks, held, sem):
+def project_kernel(order, *refs):
+    blocks, (weight, out, table_out, held, taps, staged, extra, sem) = refs[:N], refs[N:]
+    fill = pltpu.make_async_copy(weight, taps, sem.at[2 * N])
+    fill.start()
     copies = [
-        pltpu.make_async_copy(block, held.at[order[b]], sem.at[b])
-        for b, block in enumerate(blocks)
+        pltpu.make_async_copy(block, held.at[b], sem.at[b]) for b, block in enumerate(blocks)
     ]
     for copy in copies:
         copy.start()
-    for copy in copies:
-        copy.wait()
-
-
-def multiply(held, home, weight):
-    rows = jnp.concatenate(
-        [held[:, h * home : (h + 1) * home, :].reshape(N * home, HEAD) for h in range(GROUP)], axis=1
-    )
-    rows = lax.dot_general(rows, weight[...], NT, preferred_element_type=F32)
-    return rows.reshape(N, home, rows.shape[1]).astype(BF16)
-
-
-def project_kernel(count, order, *refs):
-    blocks, (weight, out, home_out, held, sem) = refs[:-5], refs[-5:]
-    fetch(order, blocks, held, sem)
-    rows = multiply(held, N * count * STEPS, weight)
-    put(out, pack(rows.astype(F32)))
-    home_out[...] = rows
-
-
-def last_kernel(counts, order, *refs):
-    parts = len(counts)
-    refs, (weight, out, table_out, held, sem) = refs[:-5], refs[-5:]
-    cut = len(refs) - (parts - 1)
-    blocks, earlier = refs[:cut], refs[cut:]
-    count = counts[-1]
-    home = N * count * STEPS
-    fetch(order, blocks, held, sem)
-    table = held[:, GROUP * home :, :].astype(F32)
+    fill.wait()
+    cols = taps.shape[0]
+    size = staged.shape[1]
+    lane = lax.broadcasted_iota(jnp.int32, (1, HOME), 1)
+    sub = lax.broadcasted_iota(jnp.int32, (N, HOME), 0)
+    table = jnp.zeros((N, HOME), F32)
+    sends, halves, codes = [], [], []
+    for first in range(0, N, AT_ONCE):
+        for copy in copies[first : first + AT_ONCE]:
+            copy.wait()
+        depth = [
+            held[first : first + AT_ONCE, h * HOME : (h + 1) * HOME, :].reshape(AT_ONCE * HOME, HEAD)
+            for h in range(GROUP)
+        ]
+        rows = lax.dot_general(
+            jnp.concatenate(depth, axis=1), taps[...], NT, preferred_element_type=F32
+        )
+        at = 0
+        for part in pack(rows.reshape(AT_ONCE, HOME, cols)):
+            staged[first : first + AT_ONCE, at : at + part.shape[1], :] = part.astype(BF16)
+            at += part.shape[1]
+        for b in range(first, first + AT_ONCE):
+            send = pltpu.make_async_copy(
+                staged.at[b], out.at[order[b], pl.ds(0, size)], sem.at[N + b]
+            )
+            send.start()
+            sends.append(send)
+            line = held[b, GROUP * HOME :, :].astype(F32)
+            table = jnp.where(sub == order[b], line[1:2], table)
+            line = line.astype(jnp.int32)
+            here = line[1:2] == (lane % CELL) // STEPS
+            codes.append(jnp.where(here, (line[0:1] * N + lane // CELL) * STEPS + lane % STEPS, -1))
+        halves.append(rows.astype(BF16))
     table_out[...] = table
-    table = table.astype(jnp.int32)
-    rows = multiply(held, home, weight)
-    cols = rows.shape[2]
     came = jnp.zeros((N * ARRIVING, cols), F32)
-    for p, c in enumerate(counts):
-        size = N * c * STEPS
-        first = sum(counts[:p])
-        lane = lax.broadcasted_iota(jnp.int32, (N, size), 1)
-        taker = table[:, 2 * p, :size]
-        slot = table[:, 2 * p + 1, :size]
-        here = slot == first + (lane // STEPS) % c
-        code = jnp.where(here, (taker * N + lane // (c * STEPS)) * STEPS + lane % STEPS, -1)
-        source = rows if p == parts - 1 else earlier[p][...]
-        group = max(1, 256 // size)
-        for e in range(0, N, group):
-            wanted = jnp.concatenate([code[e + g : e + g + 1] for g in range(group)], axis=1)
-            r = lax.broadcasted_iota(jnp.int32, (N * ARRIVING, group * size), 0)
-            pick = (r == wanted).astype(F32).astype(BF16)
-            came = came + jnp.dot(
-                pick, source[e : e + group].reshape(group * size, cols), preferred_element_type=F32
-            )
-    both = jnp.concatenate([rows.astype(F32), came.reshape(N, ARRIVING, cols)], axis=1)
-    put(out, pack(both))
-
-
-def project(counts, order, blocks, weight, earlier):
-    cols, depth = weight.shape
-    count = counts[-1]
-    home = N * count * STEPS
-    last = len(counts) == len(CHUNKS)
-    sent = home + (ARRIVING if last else 0)
-    earlier = earlier if last else []
-
-    def kernel(*refs):
-        if last:
-            last_kernel(counts, *refs)
-        else:
-            project_kernel(count, *refs)
-
-    def whole(shape):
-        return pl.BlockSpec(shape, lambda g, *_: (0,) * len(shape))
-
-    shapes = [(N, sent * cols // LANES, LANES), (N, META, LANES) if last else (N, home, cols)]
+    for g, rows in enumerate(halves):
+        wanted = jnp.concatenate(codes[g * AT_ONCE : (g + 1) * AT_ONCE], axis=1)
+        r = lax.broadcasted_iota(jnp.int32, (N * ARRIVING, wanted.shape[1]), 0)
+        pick = (r == wanted).astype(F32).astype(BF16)
+        came = came + jnp.dot(pick, rows, preferred_element_type=F32)
+    at = 0
+    for part in pack(came.reshape(N, ARRIVING, cols)):
+        extra[:, at : at + part.shape[1], :] = part.astype(BF16)
+        at += part.shape[1]
+    rest = pltpu.make_async_copy(extra, out.at[:, pl.ds(size, extra.shape[1])], sem.at[2 * N + 1])
+    rest.start()
+    sends.append(rest)
+    for send in sends:
+        send.wait()
+
+
+def project(order, blocks, weight):
+    cols = weight.shape[0]
+    packed = HOME * cols // LANES
+    added = ARRIVING * cols // LANES
+    hbm = pl.BlockSpec(memory_space=pltpu.HBM)
     return pl.pallas_call(
-        kernel,
+        project_kernel,
         grid_spec=pltpu.PrefetchScalarGridSpec(
             num_scalar_prefetch=1,
             grid=(1,),
-            in_specs=[pl.BlockSpec(memory_space=pltpu.HBM)] * len(blocks)
-            + [whole(e.shape) for e in earlier]
-            + [whole(weight.shape)],
-            out_specs=[whole(s) for s in shapes],
+            in_specs=[hbm] * (N + 1),
+            out_specs=[hbm, pl.BlockSpec((N, HOME), lambda g, *_: (0, 0))],
             scratch_shapes=[
                 pltpu.VMEM((N,) + blocks[0].shape, BF16),
-                pltpu.SemaphoreType.DMA((len(blocks),)),
+                pltpu.VMEM(weight.shape, BF16),
+                pltpu.VMEM((N, packed, LANES), BF16),
+                pltpu.VMEM((N, added, LANES), BF16),
+                pltpu.SemaphoreType.DMA((2 * N + 2,)),
             ],
         ),
         out_shape=[
-            jax.ShapeDtypeStruct(shapes[0], BF16),
-            jax.ShapeDtypeStruct(shapes[1], F32 if last else BF16),
+            jax.ShapeDtypeStruct((N, packed + added, LANES), BF16),
+            jax.ShapeDtypeStruct((N, HOME), F32),
         ],
-        compiler_params=pltpu.CompilerParams(vmem_limit_bytes=48 * 2**20),
-    )(order, *blocks, *earlier, weight)
-
-
-def finish_kernel(mine, table, *refs):
-    shares, out = refs[:-1], refs[-1]
-    rows = []
-    for got, (_, c) in zip(shares, CHUNKS, strict=True):
-        total = got[0].astype(F32)
-        for j in range(1, N):
-            total = total + got[j].astype(F32)
-        rows.append(unpack(total, total.shape[0] * LANES // out.shape[1]).astype(BF16))
-    rows = jnp.concatenate(rows, axis=0)
-    size = out.shape[0]
+        compiler_params=pltpu.CompilerParams(vmem_limit_bytes=50 * 2**20),
+    )(order, *blocks, weight)
+
+
+def finish_kernel(mine, table, got, out):
+    total = got[0].astype(F32)
+    for j in range(1, N):
+        total = total + got[j].astype(F32)
+    size, cols = out.shape
+    packed = HOME * cols // LANES
+    rows = jnp.concatenate(
+        [unpack(total[:packed], HOME), unpack(total[packed:], ARRIVING)], axis=0
+    ).astype(BF16)
     o = lax.broadcasted_iota(jnp.int32, (size, size), 0)
     col = lax.broadcasted_iota(jnp.int32, (size, size), 1)
     slots = REQ + 1
     step, j, slot = o // (N * slots), (o // slots) % N, o % slots
-    source = size - ARRIVING + j * STEPS + step
-    before = 0
-    for first, c in CHUNKS:
-        inside = (slot >= first) & (slot < first + c)
-        source = jnp.where(inside, before + j * c * STEPS + (slot - first) * STEPS + step, source)
-        before += N * c * STEPS
-    c0 = CHUNKS[0][1] * STEPS
-    line = table[:, 1, : N * c0]
+    source = jnp.where(slot < REQ, j * CELL + slot * STEPS + step, HOME + j * STEPS + step)
+    line = table[...]
     row = lax.broadcasted_iota(jnp.int32, line.shape, 0)
     line = jnp.sum(jnp.where(row == mine[0], line, 0.0), axis=0, keepdims=True)
-    r = lax.broadcasted_iota(jnp.int32, (size, N * c0), 0)
-    lane = lax.broadcasted_iota(jnp.int32, (size, N * c0), 1)
-    pick_slot = ((r // slots) % N) * c0 == lane
+    r = lax.broadcasted_iota(jnp.int32, (size, HOME), 0)
+    lane = lax.broadcasted_iota(jnp.int32, (size, HOME), 1)
+    pick_slot = ((r // slots) % N) * CELL == lane
     away = jnp.sum(jnp.where(pick_slot, line, 0.0), axis=1, keepdims=True)
     slot_of = lax.broadcasted_iota(jnp.int32, (size, 1), 0) % slots
     stays = (slot_of == REQ) | (slot_of.astype(F32) != away)
@@ -300,16 +282,15 @@
     out[...] = jnp.dot(pick, rows, preferred_element_type=F32).astype(BF16)
 
 
-def finish(mine, table, shares, cols):
+def finish(mine, table, got, cols):
     vmem = pl.BlockSpec(memory_space=pltpu.VMEM)
-    size = sum(s.shape[1] for s in shares) * LANES // cols
     return pl.pallas_call(
         finish_kernel,
-        in_specs=[pl.BlockSpec(memory_space=pltpu.SMEM), vmem] + [vmem] * len(shares),
+        in_specs=[pl.BlockSpec(memory_space=pltpu.SMEM), vmem, vmem],
         out_specs=vmem,
-        out_shape=jax.ShapeDtypeStruct((size, cols), BF16),
+        out_shape=jax.ShapeDtypeStruct((HOME + ARRIVING, cols), BF16),
         compiler_params=pltpu.CompilerParams(vmem_limit_bytes=16 * 2**20),
-    )(mine, table, *shares)
+    )(mine, table, got)
 
 
 def along_z(by):
@@ -343,15 +324,14 @@
     cache = jnp.swapaxes(latent_cache, 1, 2)
     asked = jnp.swapaxes(queries, 2, 3)
     weight = jnp.swapaxes(output_weight, 0, 1)
-    counts = tuple(c for _, c in CHUNKS)
     sent = attend(lengths, migrations, asked, cache, new_latents)
     hidden = values(across_tp(sent), value_weight)
     blocks, order = gather(hidden[0])
-    partial, table = project(counts, order, blocks, weight, [])
+    partial, table = project(order, blocks, weight)
     mine = lax.axis_index("tp").astype(jnp.int32).reshape(1)
     partial, table, mine = lax.optimization_barrier((partial, table, mine))
     shares = across_tp(partial)
-    return finish(mine, table, [shares], weight.shape[0])
+    return finish(mine, table, shares, weight.shape[0])
 
 
 def solution(mesh):

time: 113 us -> 112 us (level)
  no operation moved by 1% of the time
where the time goes in v4:
time: 112 us
  blocking collectives  57.6 us (51%)
  starting transfers between devices  26.5 us (24%)
  Pallas kernels  17.2 us (15%)
  waiting for transfers between devices  10.5 us (9%)
    all_to_all x2, blocking collectives, across_tp(): return lax.all_to_all(x, 'tp', split_axis=0, concat_axis=0, tiled=True)  57.6 us
    ppermute x8, starting transfers between devices, gather(): held += [(lax.ppermute(b, 'dp', OTHER_CORE), i ^ 1) for b, i in held]  15.1 us
    ppermute x3, starting transfers between devices, gather(): down = lax.ppermute(down, 'dp', along_z(-1))  9.69 us
    pallas_call x1, Pallas kernels, attend(): pl.pallas_call(attend_kernel, grid_spec=pltpu.PrefetchScalarGridSpec(num_...  8.41 us
    ppermute x4, waiting for transfers between devices, gather(): up = lax.ppermute(up, 'dp', along_z(1))  8.2 us
    pallas_call x1, Pallas kernels, project(): pl.pallas_call(project_kernel, grid_spec=pltpu.PrefetchScalarGridSpec(num...  6.78 us
  transfers between devices with their start and end apart: 15, of which 4 were waited for; matrix products, arithmetic and copies ran while one was open for 0% of the time, Pallas kernels for 0%

profile of v4, /device:TPU:1, one launch (start us, length us, event | category | flops | bytes accessed | tf_op | source)
XLA Modules:
  0.0 111.9 jit_solution(1511420316136065934)
XLA Ops:
  0.0 8.4 %shard_map.73 = bf16[16,272,128]{2,1,0:T(8,128)(2,1)} custom-call(s32[4]{0:T(128)} %lengths.1, s32[1,2]{1,0:T(1,128)} %moves.1, bf16[2,4,576,128]{3,2,1,0:T(8,128)(2,1)} %bitcast.21, bf16[4,576,1024]{2,1,0:T(8,128)(2,1)} %bitcast.20, bf16[2,4,576]{2,1,0:T(4,128)(2,1)} %new.1), custom_call_target="tpu_custom_call" | custom-call | tf_op jit(solution)/shard_map/pallas_call | solution.py:78
  8.4 24.4 %all_to_all.10.got = bf16[16,272,128]{2,1,0:T(8,128)(2,1)S(1)} all-to-all(bf16[16,272,128]{2,1,0:T(8,128)(2,1)} %shard_map.73), channel_id=1, replica_groups=mesh['dp'=16,'tp'=16] {'tp'}, dimensions={0} | all-to-all | bytes 2228224 | tf_op jit(solution)/shard_map/all_to_all | solution.py:320
  32.8 0.7 shard_map.74.refs_0_
  33.5 1.7 %collective-permute-start = (bf16[1040,128]{1,0:T(8,128)(2,1)S(1)}, bf16[1040,128]{1,0:T(8,128)(2,1)S(1)}, u32[]{:S(2)}, u32[]{:S(2)}) collective-permute-start(bf16[1040,128]{1,0:T(8,128)(2,1)S(1)} %shard_map.74.refs_0_), channel_id=1, source_target_pairs={{0,32},{16,48},{32,64},{48,80},{64,96},{80,112},{96,128},{112,144}... | collective-permute-start | bytes 798728 | tf_op jit(solution)/shard_map/ppermute | solution.py:310
  35.2 4.1 %collective-permute-start.1 = (bf16[1040,128]{1,0:T(8,128)(2,1)S(1)}, bf16[1040,128]{1,0:T(8,128)(2,1)S(1)}, u32[]{:S(2)}, u32[]{:S(2)}) collective-permute-start(bf16[1040,128]{1,0:T(8,128)(2,1)S(1)} %shard_map.74.refs_0_), channel_id=1, source_target_pairs={{0,224},{16,240},{32,0},{48,16},{64,32},{80,48},{96,64},{112,80},{... | collective-permute-start | bytes 798728 | tf_op jit(solution)/shard_map/ppermute | solution.py:313
  39.3 4.4 %collective-permute-done.refs_1_ = bf16[1040,128]{1,0:T(8,128)(2,1)S(1)} collective-permute-done((bf16[1040,128]{1,0:T(8,128)(2,1)S(1)}, bf16[1040,128]{1,0:T(8,128)(2,1)S(1)}, u32[]{:S(2)}, u32[]{:S(2)}) %collective-permute-start) | collective-permute-done | bytes 266272 | tf_op jit(solution)/shard_map/ppermute | solution.py:310
  43.7 2.7 %collective-permute-start.3 = (bf16[1040,128]{1,0:T(8,128)(2,1)S(1)}, bf16[1040,128]{1,0:T(8,128)(2,1)S(1)}, u32[]{:S(2)}, u32[]{:S(2)}) collective-permute-start(bf16[1040,128]{1,0:T(8,128)(2,1)S(1)} %collective-permute-done.1.refs_2_), channel_id=1, source_target_pairs={{0,224},{16,240},{32,0},{48,16},{64,32},{80,48},{96,64},{112,80},{... | collective-permute-start | bytes 798728 | tf_op jit(solution)/shard_map/ppermute | solution.py:313
  46.4 3.8 %collective-permute-done.2.refs_3_ = bf16[1040,128]{1,0:T(8,128)(2,1)S(1)} collective-permute-done((bf16[1040,128]{1,0:T(8,128)(2,1)S(1)}, bf16[1040,128]{1,0:T(8,128)(2,1)S(1)}, u32[]{:S(2)}, u32[]{:S(2)}) %collective-permute-start.2) | collective-permute-done | bytes 266272 | tf_op jit(solution)/shard_map/ppermute | solution.py:310
  50.2 0.0 collective-permute-start.4
  50.2 4.0 %collective-permute-start.7 = (bf16[1040,128]{1,0:T(8,128)(2,1)S(1)}, bf16[1040,128]{1,0:T(8,128)(2,1)S(1)}, u32[]{:S(2)}, u32[]{:S(2)}) collective-permute-start(bf16[1040,128]{1,0:T(8,128)(2,1)S(1)} %shard_map.74.refs_0_), channel_id=1, source_target_pairs={{0,16},{16,0},{32,48},{48,32},{64,80},{80,64},{96,112},{112,96},{1... | collective-permute-start | bytes 798728 | tf_op jit(solution)/shard_map/ppermute | solution.py:315
  54.2 0.0 collective-permute-start.9
  54.2 0.5 collective-permute-start.8
  54.7 3.0 %collective-permute-start.5 = (bf16[1040,128]{1,0:T(8,128)(2,1)S(1)}, bf16[1040,128]{1,0:T(8,128)(2,1)S(1)}, u32[]{:S(2)}, u32[]{:S(2)}) collective-permute-start(bf16[1040,128]{1,0:T(8,128)(2,1)S(1)} %collective-permute-done.3.refs_4_), channel_id=1, source_target_pairs={{0,224},{16,240},{32,0},{48,16},{64,32},{80,48},{96,64},{112,80},{... | collective-permute-start | bytes 798728 | tf_op jit(solution)/shard_map/ppermute | solution.py:313
  57.7 4.2 %collective-permute-start.11 = (bf16[1040,128]{1,0:T(8,128)(2,1)S(1)}, bf16[1040,128]{1,0:T(8,128)(2,1)S(1)}, u32[]{:S(2)}, u32[]{:S(2)}) collective-permute-start(bf16[1040,128]{1,0:T(8,128)(2,1)S(1)} %collective-permute-done.3.refs_4_), channel_id=1, source_target_pairs={{0,16},{16,0},{32,48},{48,32},{64,80},{80,64},{96,112},{112,96},{1... | collective-permute-start | bytes 798728 | tf_op jit(solution)/shard_map/ppermute | solution.py:315
  61.8 0.1 collective-permute-start.10
  61.9 0.4 collective-permute-start.12
  62.3 1.1 %collective-permute-done.5.refs_6_ = bf16[1040,128]{1,0:T(8,128)(2,1)S(1)} collective-permute-done((bf16[1040,128]{1,0:T(8,128)(2,1)S(1)}, bf16[1040,128]{1,0:T(8,128)(2,1)S(1)}, u32[]{:S(2)}, u32[]{:S(2)}) %collective-permute-start.5) | collective-permute-done | bytes 266272 | tf_op jit(solution)/shard_map/ppermute | solution.py:313
  63.5 0.8 collective-permute-start.13
  64.3 5.2 %collective-permute-start.14 = (bf16[1040,128]{1,0:T(8,128)(2,1)S(1)}, bf16[1040,128]{1,0:T(8,128)(2,1)}, u32[]{:S(2)}, u32[]{:S(2)}) collective-permute-start(bf16[1040,128]{1,0:T(8,128)(2,1)S(1)} %collective-permute-done.6.refs_7_), channel_id=1, source_target_pairs={{0,16},{16,0},{32,48},{48,32},{64,80},{80,64},{96,112},{112,96},{1... | collective-permute-start | bytes 798728 | tf_op jit(solution)/shard_map/ppermute | solution.py:315
  69.4 0.1 stack.67.order
  69.6 1.2 %collective-permute-done.14.refs_15_ = bf16[1040,128]{1,0:T(8,128)(2,1)} collective-permute-done((bf16[1040,128]{1,0:T(8,128)(2,1)S(1)}, bf16[1040,128]{1,0:T(8,128)(2,1)}, u32[]{:S(2)}, u32[]{:S(2)}) %collective-permute-start.14) | collective-permute-done | bytes 266272 | tf_op jit(solution)/shard_map/ppermute | solution.py:315
  70.7 6.8 %shard_map.75 = (bf16[16,560,128]{2,1,0:T(8,128)(2,1)}, f32[16,128]{1,0:T(8,128)S(1)}) custom-call(s32[16]{0:T(128)S(1)} %stack.67.order, bf16[1040,128]{1,0:T(8,128)(2,1)S(1)} %shard_map.74.refs_0_, bf16[1040,128]{1,0:T(8,128)(2,1)S(1)} %collective-permute-done.refs_1_, bf16[1040,128]{1,0:T(8,128)(2,1)S(1)} %collective-permute-done.1.refs_2_, ...), custom_call_target="tpu_custom_call" | custom-call | tf_op jit(solution)/shard_map/pallas_call | solution.py:235
  77.5 33.2 %all_to_all.11.got = bf16[16,560,128]{2,1,0:T(8,128)(2,1)S(1)} all-to-all(bf16[16,560,128]{2,1,0:T(8,128)(2,1)} %get-tuple-element.14), channel_id=1, replica_groups=mesh['dp'=16,'tp'=16] {'tp'}, dimensions={0} | all-to-all | bytes 4587520 | tf_op jit(solution)/shard_map/all_to_all | solution.py:320
  110.7 1.2 %shard_map.76 = bf16[160,448]{1,0:T(8,128)(2,1)} custom-call(s32[1]{0:T(128)} %bitcast.19.mine, f32[16,128]{1,0:T(8,128)S(1)} %get-tuple-element.13.table, bf16[16,560,128]{2,1,0:T(8,128)(2,1)S(1)} %all_to_all.11.got), custom_call_target="tpu_custom_call" | custom-call | tf_op jit(solution)/shard_map/pallas_call | solution.py:287
  (15 shorter events, 0.0 us)
Async XLA Ops:
  8.4 24.4 %copy-start = (bf16[8,512,128]{2,1,0:T(8,128)(2,1)S(1)}, bf16[8,512,128]{2,1,0:T(8,128)(2,1)}, u32[]{:S(2)}) copy-start(bf16[8,512,128]{2,1,0:T(8,128)(2,1)} %weight.1) | copy-start | bytes 3145732
  33.5 10.2 %collective-permute-start = (bf16[1040,128]{1,0:T(8,128)(2,1)S(1)}, bf16[1040,128]{1,0:T(8,128)(2,1)S(1)}, u32[]{:S(2)}, u32[]{:S(2)}) collective-permute-start(bf16[1040,128]{1,0:T(8,128)(2,1)S(1)} %shard_map.74.refs_0_), channel_id=1, source_target_pairs={{0,32},{16,48},{32,64},{48,80},{64,96},{80,112},{96,128},{112,144}... | collective-permute-start | bytes 798728 | tf_op jit(solution)/shard_map/ppermute | solution.py:310
  35.2 8.5 %collective-permute-start.1 = (bf16[1040,128]{1,0:T(8,128)(2,1)S(1)}, bf16[1040,128]{1,0:T(8,128)(2,1)S(1)}, u32[]{:S(2)}, u32[]{:S(2)}) collective-permute-start(bf16[1040,128]{1,0:T(8,128)(2,1)S(1)} %shard_map.74.refs_0_), channel_id=1, source_target_pairs={{0,224},{16,240},{32,0},{48,16},{64,32},{80,48},{96,64},{112,80},{... | collective-permute-start | bytes 798728 | tf_op jit(solution)/shard_map/ppermute | solution.py:313
  43.7 6.5 %collective-permute-start.2 = (bf16[1040,128]{1,0:T(8,128)(2,1)S(1)}, bf16[1040,128]{1,0:T(8,128)(2,1)S(1)}, u32[]{:S(2)}, u32[]{:S(2)}) collective-permute-start(bf16[1040,128]{1,0:T(8,128)(2,1)S(1)} %collective-permute-done.refs_1_), channel_id=1, source_target_pairs={{0,32},{16,48},{32,64},{48,80},{64,96},{80,112},{96,128},{112,144}... | collective-permute-start | bytes 798728 | tf_op jit(solution)/shard_map/ppermute | solution.py:310
  43.7 11.0 %collective-permute-start.3 = (bf16[1040,128]{1,0:T(8,128)(2,1)S(1)}, bf16[1040,128]{1,0:T(8,128)(2,1)S(1)}, u32[]{:S(2)}, u32[]{:S(2)}) collective-permute-start(bf16[1040,128]{1,0:T(8,128)(2,1)S(1)} %collective-permute-done.1.refs_2_), channel_id=1, source_target_pairs={{0,224},{16,240},{32,0},{48,16},{64,32},{80,48},{96,64},{112,80},{... | collective-permute-start | bytes 798728 | tf_op jit(solution)/shard_map/ppermute | solution.py:313
  50.2 7.5 %collective-permute-start.4 = (bf16[1040,128]{1,0:T(8,128)(2,1)S(1)}, bf16[1040,128]{1,0:T(8,128)(2,1)S(1)}, u32[]{:S(2)}, u32[]{:S(2)}) collective-permute-start(bf16[1040,128]{1,0:T(8,128)(2,1)S(1)} %collective-permute-done.2.refs_3_), channel_id=1, source_target_pairs={{0,32},{16,48},{32,64},{48,80},{64,96},{80,112},{96,128},{112,144}... | collective-permute-start | bytes 798728 | tf_op jit(solution)/shard_map/ppermute | solution.py:310
  50.2 7.5 %collective-permute-start.7 = (bf16[1040,128]{1,0:T(8,128)(2,1)S(1)}, bf16[1040,128]{1,0:T(8,128)(2,1)S(1)}, u32[]{:S(2)}, u32[]{:S(2)}) collective-permute-start(bf16[1040,128]{1,0:T(8,128)(2,1)S(1)} %shard_map.74.refs_0_), channel_id=1, source_target_pairs={{0,16},{16,0},{32,48},{48,32},{64,80},{80,64},{96,112},{112,96},{1... | collective-permute-start | bytes 798728 | tf_op jit(solution)/shard_map/ppermute | solution.py:315
  54.2 7.6 %collective-permute-start.9 = (bf16[1040,128]{1,0:T(8,128)(2,1)S(1)}, bf16[1040,128]{1,0:T(8,128)(2,1)S(1)}, u32[]{:S(2)}, u32[]{:S(2)}) collective-permute-start(bf16[1040,128]{1,0:T(8,128)(2,1)S(1)} %collective-permute-done.1.refs_2_), channel_id=1, source_target_pairs={{0,16},{16,0},{32,48},{48,32},{64,80},{80,64},{96,112},{112,96},{1... | collective-permute-start | bytes 798728 | tf_op jit(solution)/shard_map/ppermute | solution.py:315
  54.2 7.7 %collective-permute-start.8 = (bf16[1040,128]{1,0:T(8,128)(2,1)S(1)}, bf16[1040,128]{1,0:T(8,128)(2,1)S(1)}, u32[]{:S(2)}, u32[]{:S(2)}) collective-permute-start(bf16[1040,128]{1,0:T(8,128)(2,1)S(1)} %collective-permute-done.refs_1_), channel_id=1, source_target_pairs={{0,16},{16,0},{32,48},{48,32},{64,80},{80,64},{96,112},{112,96},{1... | collective-permute-start | bytes 798728 | tf_op jit(solution)/shard_map/ppermute | solution.py:315
  54.7 8.8 %collective-permute-start.5 = (bf16[1040,128]{1,0:T(8,128)(2,1)S(1)}, bf16[1040,128]{1,0:T(8,128)(2,1)S(1)}, u32[]{:S(2)}, u32[]{:S(2)}) collective-permute-start(bf16[1040,128]{1,0:T(8,128)(2,1)S(1)} %collective-permute-done.3.refs_4_), channel_id=1, source_target_pairs={{0,224},{16,240},{32,0},{48,16},{64,32},{80,48},{96,64},{112,80},{... | collective-permute-start | bytes 798728 | tf_op jit(solution)/shard_map/ppermute | solution.py:313
  57.6 6.6 %collective-permute-start.6 = (bf16[1040,128]{1,0:T(8,128)(2,1)S(1)}, bf16[1040,128]{1,0:T(8,128)(2,1)S(1)}, u32[]{:S(2)}, u32[]{:S(2)}) collective-permute-start(bf16[1040,128]{1,0:T(8,128)(2,1)S(1)} %collective-permute-done.4.refs_5_), channel_id=1, source_target_pairs={{0,32},{16,48},{32,64},{48,80},{64,96},{80,112},{96,128},{112,144}... | collective-permute-start | bytes 798728 | tf_op jit(solution)/shard_map/ppermute | solution.py:310
  57.7 11.9 %collective-permute-start.11 = (bf16[1040,128]{1,0:T(8,128)(2,1)S(1)}, bf16[1040,128]{1,0:T(8,128)(2,1)S(1)}, u32[]{:S(2)}, u32[]{:S(2)}) collective-permute-start(bf16[1040,128]{1,0:T(8,128)(2,1)S(1)} %collective-permute-done.3.refs_4_), channel_id=1, source_target_pairs={{0,16},{16,0},{32,48},{48,32},{64,80},{80,64},{96,112},{112,96},{1... | collective-permute-start | bytes 798728 | tf_op jit(solution)/shard_map/ppermute | solution.py:315
  61.8 7.7 %collective-permute-start.10 = (bf16[1040,128]{1,0:T(8,128)(2,1)S(1)}, bf16[1040,128]{1,0:T(8,128)(2,1)S(1)}, u32[]{:S(2)}, u32[]{:S(2)}) collective-permute-start(bf16[1040,128]{1,0:T(8,128)(2,1)S(1)} %collective-permute-done.2.refs_3_), channel_id=1, source_target_pairs={{0,16},{16,0},{32,48},{48,32},{64,80},{80,64},{96,112},{112,96},{1... | collective-permute-start | bytes 798728 | tf_op jit(solution)/shard_map/ppermute | solution.py:315
  61.9 7.6 %collective-permute-start.12 = (bf16[1040,128]{1,0:T(8,128)(2,1)S(1)}, bf16[1040,128]{1,0:T(8,128)(2,1)}, u32[]{:S(2)}, u32[]{:S(2)}) collective-permute-start(bf16[1040,128]{1,0:T(8,128)(2,1)S(1)} %collective-permute-done.4.refs_5_), channel_id=1, source_target_pairs={{0,16},{16,0},{32,48},{48,32},{64,80},{80,64},{96,112},{112,96},{1... | collective-permute-start | bytes 798728 | tf_op jit(solution)/shard_map/ppermute | solution.py:315
  63.5 6.1 %collective-permute-start.13 = (bf16[1040,128]{1,0:T(8,128)(2,1)S(1)}, bf16[1040,128]{1,0:T(8,128)(2,1)}, u32[]{:S(2)}, u32[]{:S(2)}) collective-permute-start(bf16[1040,128]{1,0:T(8,128)(2,1)S(1)} %collective-permute-done.5.refs_6_), channel_id=1, source_target_pairs={{0,16},{16,0},{32,48},{48,32},{64,80},{80,64},{96,112},{112,96},{1... | collective-permute-start | bytes 798728 | tf_op jit(solution)/shard_map/ppermute | solution.py:315
  64.3 6.5 %collective-permute-start.14 = (bf16[1040,128]{1,0:T(8,128)(2,1)S(1)}, bf16[1040,128]{1,0:T(8,128)(2,1)}, u32[]{:S(2)}, u32[]{:S(2)}) collective-permute-start(bf16[1040,128]{1,0:T(8,128)(2,1)S(1)} %collective-permute-done.6.refs_7_), channel_id=1, source_target_pairs={{0,16},{16,0},{32,48},{48,32},{64,80},{80,64},{96,112},{112,96},{1... | collective-permute-start | bytes 798728 | tf_op jit(solution)/shard_map/ppermute | solution.py:315

commit v5 on v4

--- a/solution.py
+++ b/solution.py
@@ -20,7 +20,7 @@
 CHUNKS = ((0, 4),)
 CELL = REQ * STEPS
 HOME = N * CELL
-AT_ONCE = 8
+AT_ONCE = 16
 ARRIVING = N * STEPS
 TOGETHER = 2
 F32 = jnp.float32

time: 112 us -> 112 us (level)
  no operation moved by 1% of the time
where the time goes in v5:
time: 112 us
  blocking collectives  57.6 us (51%)
  starting transfers between devices  26.5 us (24%)
  Pallas kernels  17.4 us (16%)
  waiting for transfers between devices  10.5 us (9%)
    all_to_all x2, blocking collectives, across_tp(): return lax.all_to_all(x, 'tp', split_axis=0, concat_axis=0, tiled=True)  57.6 us
    ppermute x8, starting transfers between devices, gather(): held += [(lax.ppermute(b, 'dp', OTHER_CORE), i ^ 1) for b, i in held]  15.1 us
    ppermute x3, starting transfers between devices, gather(): down = lax.ppermute(down, 'dp', along_z(-1))  9.69 us
    pallas_call x1, Pallas kernels, attend(): pl.pallas_call(attend_kernel, grid_spec=pltpu.PrefetchScalarGridSpec(num_...  8.41 us
    ppermute x4, waiting for transfers between devices, gather(): up = lax.ppermute(up, 'dp', along_z(1))  8.2 us
    pallas_call x1, Pallas kernels, project(): pl.pallas_call(project_kernel, grid_spec=pltpu.PrefetchScalarGridSpec(num...  7.05 us
  transfers between devices with their start and end apart: 15, of which 4 were waited for; matrix products, arithmetic and copies ran while one was open for 0% of the time, Pallas kernels for 0%

profile of v5, /device:TPU:1, one launch (start us, length us, event | category | flops | bytes accessed | tf_op | source)
XLA Modules:
  0.0 112.2 jit_solution(4626045360541334677)
XLA Ops:
  0.0 8.4 %shard_map.73 = bf16[16,272,128]{2,1,0:T(8,128)(2,1)} custom-call(s32[4]{0:T(128)} %lengths.1, s32[1,2]{1,0:T(1,128)} %moves.1, bf16[2,4,576,128]{3,2,1,0:T(8,128)(2,1)} %bitcast.21, bf16[4,576,1024]{2,1,0:T(8,128)(2,1)} %bitcast.20, bf16[2,4,576]{2,1,0:T(4,128)(2,1)} %new.1), custom_call_target="tpu_custom_call" | custom-call | tf_op jit(solution)/shard_map/pallas_call | solution.py:78
  8.4 24.4 %all_to_all.10.got = bf16[16,272,128]{2,1,0:T(8,128)(2,1)S(1)} all-to-all(bf16[16,272,128]{2,1,0:T(8,128)(2,1)} %shard_map.73), channel_id=1, replica_groups=mesh['dp'=16,'tp'=16] {'tp'}, dimensions={0} | all-to-all | bytes 2228224 | tf_op jit(solution)/shard_map/all_to_all | solution.py:320
  32.8 0.7 shard_map.74.refs_0_
  33.5 1.7 %collective-permute-start = (bf16[1040,128]{1,0:T(8,128)(2,1)S(1)}, bf16[1040,128]{1,0:T(8,128)(2,1)S(1)}, u32[]{:S(2)}, u32[]{:S(2)}) collective-permute-start(bf16[1040,128]{1,0:T(8,128)(2,1)S(1)} %shard_map.74.refs_0_), channel_id=1, source_target_pairs={{0,32},{16,48},{32,64},{48,80},{64,96},{80,112},{96,128},{112,144}... | collective-permute-start | bytes 798728 | tf_op jit(solution)/shard_map/ppermute | solution.py:310
  35.2 4.1 %collective-permute-start.1 = (bf16[1040,128]{1,0:T(8,128)(2,1)S(1)}, bf16[1040,128]{1,0:T(8,128)(2,1)S(1)}, u32[]{:S(2)}, u32[]{:S(2)}) collective-permute-start(bf16[1040,128]{1,0:T(8,128)(2,1)S(1)} %shard_map.74.refs_0_), channel_id=1, source_target_pairs={{0,224},{16,240},{32,0},{48,16},{64,32},{80,48},{96,64},{112,80},{... | collective-permute-start | bytes 798728 | tf_op jit(solution)/shard_map/ppermute | solution.py:313
  39.3 4.4 %collective-permute-done.refs_1_ = bf16[1040,128]{1,0:T(8,128)(2,1)S(1)} collective-permute-done((bf16[1040,128]{1,0:T(8,128)(2,1)S(1)}, bf16[1040,128]{1,0:T(8,128)(2,1)S(1)}, u32[]{:S(2)}, u32[]{:S(2)}) %collective-permute-start) | collective-permute-done | bytes 266272 | tf_op jit(solution)/shard_map/ppermute | solution.py:310
  43.7 2.7 %collective-permute-start.3 = (bf16[1040,128]{1,0:T(8,128)(2,1)S(1)}, bf16[1040,128]{1,0:T(8,128)(2,1)S(1)}, u32[]{:S(2)}, u32[]{:S(2)}) collective-permute-start(bf16[1040,128]{1,0:T(8,128)(2,1)S(1)} %collective-permute-done.1.refs_2_), channel_id=1, source_target_pairs={{0,224},{16,240},{32,0},{48,16},{64,32},{80,48},{96,64},{112,80},{... | collective-permute-start | bytes 798728 | tf_op jit(solution)/shard_map/ppermute | solution.py:313
  46.4 3.8 %collective-permute-done.2.refs_3_ = bf16[1040,128]{1,0:T(8,128)(2,1)S(1)} collective-permute-done((bf16[1040,128]{1,0:T(8,128)(2,1)S(1)}, bf16[1040,128]{1,0:T(8,128)(2,1)S(1)}, u32[]{:S(2)}, u32[]{:S(2)}) %collective-permute-start.2) | collective-permute-done | bytes 266272 | tf_op jit(solution)/shard_map/ppermute | solution.py:310
  50.2 4.0 %collective-permute-start.7 = (bf16[1040,128]{1,0:T(8,128)(2,1)S(1)}, bf16[1040,128]{1,0:T(8,128)(2,1)S(1)}, u32[]{:S(2)}, u32[]{:S(2)}) collective-permute-start(bf16[1040,128]{1,0:T(8,128)(2,1)S(1)} %shard_map.74.refs_0_), channel_id=1, source_target_pairs={{0,16},{16,0},{32,48},{48,32},{64,80},{80,64},{96,112},{112,96},{1... | collective-permute-start | bytes 798728 | tf_op jit(solution)/shard_map/ppermute | solution.py:315
  54.2 0.0 collective-permute-start.9
  54.2 0.5 collective-permute-start.8
  54.7 0.0 collective-permute-done.3.refs_4_
  54.7 3.0 %collective-permute-start.5 = (bf16[1040,128]{1,0:T(8,128)(2,1)S(1)}, bf16[1040,128]{1,0:T(8,128)(2,1)S(1)}, u32[]{:S(2)}, u32[]{:S(2)}) collective-permute-start(bf16[1040,128]{1,0:T(8,128)(2,1)S(1)} %collective-permute-done.3.refs_4_), channel_id=1, source_target_pairs={{0,224},{16,240},{32,0},{48,16},{64,32},{80,48},{96,64},{112,80},{... | collective-permute-start | bytes 798728 | tf_op jit(solution)/shard_map/ppermute | solution.py:313
  57.7 4.2 %collective-permute-start.11 = (bf16[1040,128]{1,0:T(8,128)(2,1)S(1)}, bf16[1040,128]{1,0:T(8,128)(2,1)S(1)}, u32[]{:S(2)}, u32[]{:S(2)}) collective-permute-start(bf16[1040,128]{1,0:T(8,128)(2,1)S(1)} %collective-permute-done.3.refs_4_), channel_id=1, source_target_pairs={{0,16},{16,0},{32,48},{48,32},{64,80},{80,64},{96,112},{112,96},{1... | collective-permute-start | bytes 798728 | tf_op jit(solution)/shard_map/ppermute | solution.py:315
  61.8 0.1 collective-permute-start.10
  61.9 0.4 collective-permute-start.12
  62.3 1.1 %collective-permute-done.5.refs_6_ = bf16[1040,128]{1,0:T(8,128)(2,1)S(1)} collective-permute-done((bf16[1040,128]{1,0:T(8,128)(2,1)S(1)}, bf16[1040,128]{1,0:T(8,128)(2,1)S(1)}, u32[]{:S(2)}, u32[]{:S(2)}) %collective-permute-start.5) | collective-permute-done | bytes 266272 | tf_op jit(solution)/shard_map/ppermute | solution.py:313
  63.5 0.8 collective-permute-start.13
  64.3 5.2 %collective-permute-start.14 = (bf16[1040,128]{1,0:T(8,128)(2,1)S(1)}, bf16[1040,128]{1,0:T(8,128)(2,1)}, u32[]{:S(2)}, u32[]{:S(2)}) collective-permute-start(bf16[1040,128]{1,0:T(8,128)(2,1)S(1)} %collective-permute-done.6.refs_7_), channel_id=1, source_target_pairs={{0,16},{16,0},{32,48},{48,32},{64,80},{80,64},{96,112},{112,96},{1... | collective-permute-start | bytes 798728 | tf_op jit(solution)/shard_map/ppermute | solution.py:315
  69.4 0.1 stack.67.order
  69.6 1.2 %collective-permute-done.14.refs_15_ = bf16[1040,128]{1,0:T(8,128)(2,1)} collective-permute-done((bf16[1040,128]{1,0:T(8,128)(2,1)S(1)}, bf16[1040,128]{1,0:T(8,128)(2,1)}, u32[]{:S(2)}, u32[]{:S(2)}) %collective-permute-start.14) | collective-permute-done | bytes 266272 | tf_op jit(solution)/shard_map/ppermute | solution.py:315
  70.7 7.0 %shard_map.75 = (bf16[16,560,128]{2,1,0:T(8,128)(2,1)}, f32[16,128]{1,0:T(8,128)S(1)}) custom-call(s32[16]{0:T(128)S(1)} %stack.67.order, bf16[1040,128]{1,0:T(8,128)(2,1)S(1)} %shard_map.74.refs_0_, bf16[1040,128]{1,0:T(8,128)(2,1)S(1)} %collective-permute-done.refs_1_, bf16[1040,128]{1,0:T(8,128)(2,1)S(1)} %collective-permute-done.1.refs_2_, ...), custom_call_target="tpu_custom_call" | custom-call | tf_op jit(solution)/shard_map/pallas_call | solution.py:235
  77.8 33.2 %all_to_all.11.got = bf16[16,560,128]{2,1,0:T(8,128)(2,1)S(1)} all-to-all(bf16[16,560,128]{2,1,0:T(8,128)(2,1)} %get-tuple-element.14), channel_id=1, replica_groups=mesh['dp'=16,'tp'=16] {'tp'}, dimensions={0} | all-to-all | bytes 4587520 | tf_op jit(solution)/shard_map/all_to_all | solution.py:320
  111.0 1.2 %shard_map.76 = bf16[160,448]{1,0:T(8,128)(2,1)} custom-call(s32[1]{0:T(128)} %bitcast.19.mine, f32[16,128]{1,0:T(8,128)S(1)} %get-tuple-element.13.table, bf16[16,560,128]{2,1,0:T(8,128)(2,1)S(1)} %all_to_all.11.got), custom_call_target="tpu_custom_call" | custom-call | tf_op jit(solution)/shard_map/pallas_call | solution.py:287
  (15 shorter events, 0.0 us)
Async XLA Ops:
  8.4 24.4 %copy-start = (bf16[8,512,128]{2,1,0:T(8,128)(2,1)S(1)}, bf16[8,512,128]{2,1,0:T(8,128)(2,1)}, u32[]{:S(2)}) copy-start(bf16[8,512,128]{2,1,0:T(8,128)(2,1)} %weight.1) | copy-start | bytes 3145732
  33.5 10.2 %collective-permute-start = (bf16[1040,128]{1,0:T(8,128)(2,1)S(1)}, bf16[1040,128]{1,0:T(8,128)(2,1)S(1)}, u32[]{:S(2)}, u32[]{:S(2)}) collective-permute-start(bf16[1040,128]{1,0:T(8,128)(2,1)S(1)} %shard_map.74.refs_0_), channel_id=1, source_target_pairs={{0,32},{16,48},{32,64},{48,80},{64,96},{80,112},{96,128},{112,144}... | collective-permute-start | bytes 798728 | tf_op jit(solution)/shard_map/ppermute | solution.py:310
  35.2 8.5 %collective-permute-start.1 = (bf16[1040,128]{1,0:T(8,128)(2,1)S(1)}, bf16[1040,128]{1,0:T(8,128)(2,1)S(1)}, u32[]{:S(2)}, u32[]{:S(2)}) collective-permute-start(bf16[1040,128]{1,0:T(8,128)(2,1)S(1)} %shard_map.74.refs_0_), channel_id=1, source_target_pairs={{0,224},{16,240},{32,0},{48,16},{64,32},{80,48},{96,64},{112,80},{... | collective-permute-start | bytes 798728 | tf_op jit(solution)/shard_map/ppermute | solution.py:313
  43.7 6.5 %collective-permute-start.2 = (bf16[1040,128]{1,0:T(8,128)(2,1)S(1)}, bf16[1040,128]{1,0:T(8,128)(2,1)S(1)}, u32[]{:S(2)}, u32[]{:S(2)}) collective-permute-start(bf16[1040,128]{1,0:T(8,128)(2,1)S(1)} %collective-permute-done.refs_1_), channel_id=1, source_target_pairs={{0,32},{16,48},{32,64},{48,80},{64,96},{80,112},{96,128},{112,144}... | collective-permute-start | bytes 798728 | tf_op jit(solution)/shard_map/ppermute | solution.py:310
  43.7 11.0 %collective-permute-start.3 = (bf16[1040,128]{1,0:T(8,128)(2,1)S(1)}, bf16[1040,128]{1,0:T(8,128)(2,1)S(1)}, u32[]{:S(2)}, u32[]{:S(2)}) collective-permute-start(bf16[1040,128]{1,0:T(8,128)(2,1)S(1)} %collective-permute-done.1.refs_2_), channel_id=1, source_target_pairs={{0,224},{16,240},{32,0},{48,16},{64,32},{80,48},{96,64},{112,80},{... | collective-permute-start | bytes 798728 | tf_op jit(solution)/shard_map/ppermute | solution.py:313
  50.2 7.5 %collective-permute-start.4 = (bf16[1040,128]{1,0:T(8,128)(2,1)S(1)}, bf16[1040,128]{1,0:T(8,128)(2,1)S(1)}, u32[]{:S(2)}, u32[]{:S(2)}) collective-permute-start(bf16[1040,128]{1,0:T(8,128)(2,1)S(1)} %collective-permute-done.2.refs_3_), channel_id=1, source_target_pairs={{0,32},{16,48},{32,64},{48,80},{64,96},{80,112},{96,128},{112,144}... | collective-permute-start | bytes 798728 | tf_op jit(solution)/shard_map/ppermute | solution.py:310
  50.2 7.5 %collective-permute-start.7 = (bf16[1040,128]{1,0:T(8,128)(2,1)S(1)}, bf16[1040,128]{1,0:T(8,128)(2,1)S(1)}, u32[]{:S(2)}, u32[]{:S(2)}) collective-permute-start(bf16[1040,128]{1,0:T(8,128)(2,1)S(1)} %shard_map.74.refs_0_), channel_id=1, source_target_pairs={{0,16},{16,0},{32,48},{48,32},{64,80},{80,64},{96,112},{112,96},{1... | collective-permute-start | bytes 798728 | tf_op jit(solution)/shard_map/ppermute | solution.py:315
  54.2 7.6 %collective-permute-start.9 = (bf16[1040,128]{1,0:T(8,128)(2,1)S(1)}, bf16[1040,128]{1,0:T(8,128)(2,1)S(1)}, u32[]{:S(2)}, u32[]{:S(2)}) collective-permute-start(bf16[1040,128]{1,0:T(8,128)(2,1)S(1)} %collective-permute-done.1.refs_2_), channel_id=1, source_target_pairs={{0,16},{16,0},{32,48},{48,32},{64,80},{80,64},{96,112},{112,96},{1... | collective-permute-start | bytes 798728 | tf_op jit(solution)/shard_map/ppermute | solution.py:315
  54.2 7.7 %collective-permute-start.8 = (bf16[1040,128]{1,0:T(8,128)(2,1)S(1)}, bf16[1040,128]{1,0:T(8,128)(2,1)S(1)}, u32[]{:S(2)}, u32[]{:S(2)}) collective-permute-start(bf16[1040,128]{1,0:T(8,128)(2,1)S(1)} %collective-permute-done.refs_1_), channel_id=1, source_target_pairs={{0,16},{16,0},{32,48},{48,32},{64,80},{80,64},{96,112},{112,96},{1... | collective-permute-start | bytes 798728 | tf_op jit(solution)/shard_map/ppermute | solution.py:315
  54.7 8.8 %collective-permute-start.5 = (bf16[1040,128]{1,0:T(8,128)(2,1)S(1)}, bf16[1040,128]{1,0:T(8,128)(2,1)S(1)}, u32[]{:S(2)}, u32[]{:S(2)}) collective-permute-start(bf16[1040,128]{1,0:T(8,128)(2,1)S(1)} %collective-permute-done.3.refs_4_), channel_id=1, source_target_pairs={{0,224},{16,240},{32,0},{48,16},{64,32},{80,48},{96,64},{112,80},{... | collective-permute-start | bytes 798728 | tf_op jit(solution)/shard_map/ppermute | solution.py:313
  57.6 6.6 %collective-permute-start.6 = (bf16[1040,128]{1,0:T(8,128)(2,1)S(1)}, bf16[1040,128]{1,0:T(8,128)(2,1)S(1)}, u32[]{:S(2)}, u32[]{:S(2)}) collective-permute-start(bf16[1040,128]{1,0:T(8,128)(2,1)S(1)} %collective-permute-done.4.refs_5_), channel_id=1, source_target_pairs={{0,32},{16,48},{32,64},{48,80},{64,96},{80,112},{96,128},{112,144}... | collective-permute-start | bytes 798728 | tf_op jit(solution)/shard_map/ppermute | solution.py:310
  57.7 11.9 %collective-permute-start.11 = (bf16[1040,128]{1,0:T(8,128)(2,1)S(1)}, bf16[1040,128]{1,0:T(8,128)(2,1)S(1)}, u32[]{:S(2)}, u32[]{:S(2)}) collective-permute-start(bf16[1040,128]{1,0:T(8,128)(2,1)S(1)} %collective-permute-done.3.refs_4_), channel_id=1, source_target_pairs={{0,16},{16,0},{32,48},{48,32},{64,80},{80,64},{96,112},{112,96},{1... | collective-permute-start | bytes 798728 | tf_op jit(solution)/shard_map/ppermute | solution.py:315
  61.8 7.7 %collective-permute-start.10 = (bf16[1040,128]{1,0:T(8,128)(2,1)S(1)}, bf16[1040,128]{1,0:T(8,128)(2,1)S(1)}, u32[]{:S(2)}, u32[]{:S(2)}) collective-permute-start(bf16[1040,128]{1,0:T(8,128)(2,1)S(1)} %collective-permute-done.2.refs_3_), channel_id=1, source_target_pairs={{0,16},{16,0},{32,48},{48,32},{64,80},{80,64},{96,112},{112,96},{1... | collective-permute-start | bytes 798728 | tf_op jit(solution)/shard_map/ppermute | solution.py:315
  61.9 7.6 %collective-permute-start.12 = (bf16[1040,128]{1,0:T(8,128)(2,1)S(1)}, bf16[1040,128]{1,0:T(8,128)(2,1)}, u32[]{:S(2)}, u32[]{:S(2)}) collective-permute-start(bf16[1040,128]{1,0:T(8,128)(2,1)S(1)} %collective-permute-done.4.refs_5_), channel_id=1, source_target_pairs={{0,16},{16,0},{32,48},{48,32},{64,80},{80,64},{96,112},{112,96},{1... | collective-permute-start | bytes 798728 | tf_op jit(solution)/shard_map/ppermute | solution.py:315
  63.5 6.1 %collective-permute-start.13 = (bf16[1040,128]{1,0:T(8,128)(2,1)S(1)}, bf16[1040,128]{1,0:T(8,128)(2,1)}, u32[]{:S(2)}, u32[]{:S(2)}) collective-permute-start(bf16[1040,128]{1,0:T(8,128)(2,1)S(1)} %collective-permute-done.5.refs_6_), channel_id=1, source_target_pairs={{0,16},{16,0},{32,48},{48,32},{64,80},{80,64},{96,112},{112,96},{1... | collective-permute-start | bytes 798728 | tf_op jit(solution)/shard_map/ppermute | solution.py:315
  64.3 6.5 %collective-permute-start.14 = (bf16[1040,128]{1,0:T(8,128)(2,1)S(1)}, bf16[1040,128]{1,0:T(8,128)(2,1)}, u32[]{:S(2)}, u32[]{:S(2)}) collective-permute-start(bf16[1040,128]{1,0:T(8,128)(2,1)S(1)} %collective-permute-done.6.refs_7_), channel_id=1, source_target_pairs={{0,16},{16,0},{32,48},{48,32},{64,80},{80,64},{96,112},{112,96},{1... | collective-permute-start | bytes 798728 | tf_op jit(solution)/shard_map/ppermute | solution.py:315
